TPU v7x, 32 devices: a whole 2x2x4 slice. The times are simulated.
32 devices in a mesh: layer: 8 (over y, x, core), rows: 4 (over z).
Axes of the slice: x: 2, y: 2, z: 4, core: 2. Of those that a mesh axis runs over, the one named last changes fastest.
Arguments:
- weights: bfloat16 [64, 32, 288], P('layer'), may hold values from -0.375 to 0.375
- image: float32 [3, 32, 64, 128], P(None, None, 'rows'), may hold values from -6 to 6
- guess: float32 [16, 3, 32, 64, 128], P('layer', None, None, 'rows'), may hold values from -6 to 6
Outputs:
- corrected: float32 [16, 3, 32, 64, 128], P('layer', None, None, 'rows')
All inputs are finite; a program needn't handle non-finite values.
Results may differ from a plain program's by a relative error of at most 0.009.
Values may be sent and summed in bfloat16 or wider, within the bound.
A program may use at most 64 MiB of HBM per device.

v0:
```python
import jax
import jax.numpy as jnp
from jax import lax
from jax.sharding import PartitionSpec as P

M = 4


step_size = 0.125


def extended_2(block, sides, width):
    for axis, dim in sides:
        count = lax.axis_size(axis)
        forward = [(i, i + 1) for i in range(count - 1)]
        backward = [(target, source) for source, target in forward]
        low = lax.ppermute(
            lax.slice_in_dim(block, block.shape[dim] - width, None, axis=dim), axis, forward
        )
        high = lax.ppermute(lax.slice_in_dim(block, 0, width, axis=dim), axis, backward)
        block = jnp.concatenate([low, block, high], axis=dim)
    return block


def passed_along(value, axis, by):
    size = lax.axis_size(axis)
    pairs = [(i, i + by) for i in range(size) if 0 <= i + by < size]
    return lax.ppermute(value, axis, pairs)


def convolve(extended, matrices):
    padded = jnp.pad(extended, ((0, 0), (0, 0), (0, 0), (0, 0), (1, 1)))
    height = extended.shape[3] - 2
    breadth = extended.shape[4]
    patches = jnp.concatenate(
        [
            padded[:, :, :, row_off : row_off + height, col_off : col_off + breadth]
            for row_off in range(3)
            for col_off in range(3)
        ],
        axis=2,
    )
    return jnp.einsum("iok,inkrw->inorw", matrices, patches, preferred_element_type=jnp.float32)


def edge_rows(field, depth):
    return jnp.concatenate([field[..., :depth, :], field[..., -depth:, :]], axis=-2)


def attach(field, framed, depth):
    return jnp.concatenate([framed[..., :depth, :], field, framed[..., -depth:, :]], axis=-2)


def relax_halo(field):
    lowered = field.astype(jnp.bfloat16)
    framed = extended_2(edge_rows(lowered, 1), (("rows", 3),), 1)
    return attach(lowered, framed, 1)


def relax(anchors, grouped, stride):
    opening = convolve(relax_halo(anchors), grouped[:, 0])
    current = anchors + stride * jnp.tanh(opening)
    for layer in range(1, M):
        current = current + stride * jnp.tanh(convolve(relax_halo(current), grouped[:, layer]))
    return current - (anchors + M * stride * jnp.tanh(opening))


def advance(incoming, defects, coarse_w, stride):
    levels = coarse_w.shape[0]
    results = []
    current = incoming
    for point in range(levels):
        lowered = current.astype(jnp.bfloat16)[None]
        framed = extended_2(edge_rows(lowered, 1), (("rows", 3),), 1)
        rimmed = attach(lowered, framed, 1)
        current = (
            current
            + M * stride * jnp.tanh(convolve(rimmed, coarse_w[point][None])[0])
            + defects[point]
        )
        results.append(current)
    return jnp.stack(results)


def per_device(weights, image, guess):
    layers_dev = weights.shape[0]
    levels = layers_dev // M
    sections = lax.axis_size("layer")
    grouped = weights.reshape(levels, M, weights.shape[1], weights.shape[2])
    coarse_w = grouped[:, 0]
    section = lax.axis_index("layer")
    previous = passed_along(guess[levels - 1], "layer", 1)
    opening_state = jnp.where(section == 0, image, previous)
    anchors = jnp.concatenate([opening_state[None], guess[:-1]], axis=0)
    defects = relax(anchors, grouped, step_size)

    def sweep(index, carry):
        incoming, results = carry
        fresh = advance(incoming, defects, coarse_w, step_size)
        sent = passed_along(fresh[levels - 1], "layer", 1)
        return (jnp.where(section == 0, image, sent), fresh)

    _, corrected = lax.fori_loop(0, sections, sweep, (opening_state, jnp.zeros_like(guess)))
    return corrected


def solution(mesh):
    return jax.shard_map(
        per_device,
        mesh=mesh,
        in_specs=(
            P("layer", None, None),
            P(None, None, "rows", None),
            P("layer", None, None, "rows", None),
        ),
        out_specs=P("layer", None, None, "rows", None),
        check_vma=False,
    )
```

profile of v0, /device:TPU:28, one launch (start us, length us, event | category | flops | bytes accessed | tf_op | source)
XLA Modules:
  0.0 368.3 jit_solution(679065430955476836)
XLA Ops:
  4.1 12.1 %collective-permute-done.5 = f32[3,32,16,128]{3,1,2,0:T(8,128)} collective-permute-done((f32[3,32,16,128]{3,1,2,0:T(8,128)S(1)}, f32[3,32,16,128]{3,1,2,0:T(8,128)}, u32[]{:S(2)}, u32[]{:S(2)}) %collective-permute-start.5) | collective-permute-done | bytes 786464 | tf_op jit(solution)/shard_map/ppermute | solution.py:28
  19.9 4.5 %collective-permute-start.7 = (bf16[2,3,32,1,128]{4,2,3,1,0:T(8,128)(2,1)S(1)}, bf16[2,3,32,1,128]{4,2,3,1,0:T(8,128)(2,1)S(1)}, u32[]{:S(2)}, u32[]{:S(2)}) collective-permute-start(bf16[2,3,32,1,128]{4,2,3,1,0:T(8,128)(2,1)S(1)} %get-tuple-element.136), channel_id=1, source_target_pairs={{1,0},{2,1},{3,2},{5,4},{6,5},{7,6},{9,8},{10,9},{11,10},{13,12},{... | collective-permute-start | bytes 147464 | tf_op jit(solution)/shard_map/ppermute | solution.py:20
  32.3 4.9 %collective-permute-start.9 = (bf16[2,3,32,1,128]{4,2,3,1,0:T(8,128)(2,1)S(1)}, bf16[2,3,32,1,128]{4,2,3,1,0:T(8,128)(2,1)S(1)}, u32[]{:S(2)}, u32[]{:S(2)}) collective-permute-start(bf16[2,3,32,1,128]{4,2,3,1,0:T(8,128)(2,1)S(1)} %get-tuple-element.134), channel_id=1, source_target_pairs={{1,0},{2,1},{3,2},{5,4},{6,5},{7,6},{9,8},{10,9},{11,10},{13,12},{... | collective-permute-start | bytes 147464 | tf_op jit(solution)/shard_map/ppermute | solution.py:20
  44.8 5.1 %collective-permute-start.11 = (bf16[2,3,32,1,128]{4,2,3,1,0:T(8,128)(2,1)S(1)}, bf16[2,3,32,1,128]{4,2,3,1,0:T(8,128)(2,1)S(1)}, u32[]{:S(2)}, u32[]{:S(2)}) collective-permute-start(bf16[2,3,32,1,128]{4,2,3,1,0:T(8,128)(2,1)S(1)} %get-tuple-element.132), channel_id=1, source_target_pairs={{1,0},{2,1},{3,2},{5,4},{6,5},{7,6},{9,8},{10,9},{11,10},{13,12},{... | collective-permute-start | bytes 147464 | tf_op jit(solution)/shard_map/ppermute | solution.py:20
  58.5 4.9 %collective-permute-start.13 = (bf16[2,3,32,1,128]{4,2,3,1,0:T(8,128)(2,1)S(1)}, bf16[2,3,32,1,128]{4,2,3,1,0:T(8,128)(2,1)S(1)}, u32[]{:S(2)}, u32[]{:S(2)}) collective-permute-start(bf16[2,3,32,1,128]{4,2,3,1,0:T(8,128)(2,1)S(1)} %get-tuple-element.130), channel_id=1, source_target_pairs={{1,0},{2,1},{3,2},{5,4},{6,5},{7,6},{9,8},{10,9},{11,10},{13,12},{... | collective-permute-start | bytes 147464 | tf_op jit(solution)/shard_map/ppermute | solution.py:20
  70.5 294.3 %while.14 = (s32[]{:T(128)}, f32[3,32,16,128]{3,1,2,0:T(8,128)S(1)}, f32[2,3,32,16,128]{4,2,3,1,0:T(8,128)}, pred[]{:T(512)}, bf16[2,32,288]{2,1,0:T(8,128)(2,1)...) while((s32[]{:T(128)}, f32[3,32,16,128]{3,1,2,0:T(8,128)S(1)}, ...), condition=%wide.region_1.2_spmd, body=%wide.region_0.1_spmd.sunk | while | flops 237585408 | bytes 43415352 | solution.py:103
  70.6 4.2 %collective-permute-start = (bf16[1,3,32,1,128]{4,2,3,1,0:T(8,128)(2,1)S(1)}, bf16[1,3,32,1,128]{4,2,3,1,0:T(8,128)(2,1)S(1)}, u32[]{:S(2)}, u32[]{:S(2)}) collective-permute-start(bf16[1,3,32,1,128]{4,2,3,1,0:T(8,128)(2,1)S(1)} %get-tuple-element.188), channel_id=1, source_target_pairs={{1,0},{2,1},{3,2},{5,4},{6,5},{7,6},{9,8},{10,9},{11,10},{13,12},{... | collective-permute-start | bytes 73736 | tf_op jit(solution)/shard_map/while/body/eval_jaxpr/ppermute | solution.py:20
  76.3 4.2 %collective-permute-done.1 = bf16[1,3,32,1,128]{4,2,3,1,0:T(8,128)(2,1)S(1)} collective-permute-done((bf16[1,3,32,1,128]{4,2,3,1,0:T(8,128)(2,1)S(1)}, bf16[1,3,32,1,128]{4,2,3,1,0:T(8,128)(2,1)S(1)}, u32[]{:S(2)}, u32[]{:S(2)}) %collective-permute-start.1) | collective-permute-done | bytes 24608 | tf_op jit(solution)/shard_map/while/body/eval_jaxpr/ppermute | solution.py:17
  88.5 4.2 %collective-permute-done.3 = bf16[1,3,32,1,128]{4,2,3,1,0:T(8,128)(2,1)S(1)} collective-permute-done((bf16[1,3,32,1,128]{4,2,3,1,0:T(8,128)(2,1)S(1)}, bf16[1,3,32,1,128]{4,2,3,1,0:T(8,128)(2,1)S(1)}, u32[]{:S(2)}, u32[]{:S(2)}) %collective-permute-start.3) | collective-permute-done | bytes 24608 | tf_op jit(solution)/shard_map/while/body/eval_jaxpr/ppermute | solution.py:17
  98.5 11.0 %collective-permute-done.4 = f32[3,32,16,128]{3,1,2,0:T(8,128)} collective-permute-done((f32[3,32,16,128]{3,1,2,0:T(8,128)S(1)}, f32[3,32,16,128]{3,1,2,0:T(8,128)}, u32[]{:S(2)}, u32[]{:S(2)}) %collective-permute-start.4) | collective-permute-done | bytes 786464 | tf_op jit(solution)/shard_map/while/body/eval_jaxpr/ppermute | solution.py:28
  116.3 4.2 %collective-permute-done.1 = bf16[1,3,32,1,128]{4,2,3,1,0:T(8,128)(2,1)S(1)} collective-permute-done((bf16[1,3,32,1,128]{4,2,3,1,0:T(8,128)(2,1)S(1)}, bf16[1,3,32,1,128]{4,2,3,1,0:T(8,128)(2,1)S(1)}, u32[]{:S(2)}, u32[]{:S(2)}) %collective-permute-start.1) | collective-permute-done | bytes 24608 | tf_op jit(solution)/shard_map/while/body/eval_jaxpr/ppermute | solution.py:17
  126.5 4.2 %collective-permute-done.3 = bf16[1,3,32,1,128]{4,2,3,1,0:T(8,128)(2,1)S(1)} collective-permute-done((bf16[1,3,32,1,128]{4,2,3,1,0:T(8,128)(2,1)S(1)}, bf16[1,3,32,1,128]{4,2,3,1,0:T(8,128)(2,1)S(1)}, u32[]{:S(2)}, u32[]{:S(2)}) %collective-permute-start.3) | collective-permute-done | bytes 24608 | tf_op jit(solution)/shard_map/while/body/eval_jaxpr/ppermute | solution.py:17
  136.5 11.0 %collective-permute-done.4 = f32[3,32,16,128]{3,1,2,0:T(8,128)} collective-permute-done((f32[3,32,16,128]{3,1,2,0:T(8,128)S(1)}, f32[3,32,16,128]{3,1,2,0:T(8,128)}, u32[]{:S(2)}, u32[]{:S(2)}) %collective-permute-start.4) | collective-permute-done | bytes 786464 | tf_op jit(solution)/shard_map/while/body/eval_jaxpr/ppermute | solution.py:28
  152.3 4.2 %collective-permute-done.1 = bf16[1,3,32,1,128]{4,2,3,1,0:T(8,128)(2,1)S(1)} collective-permute-done((bf16[1,3,32,1,128]{4,2,3,1,0:T(8,128)(2,1)S(1)}, bf16[1,3,32,1,128]{4,2,3,1,0:T(8,128)(2,1)S(1)}, u32[]{:S(2)}, u32[]{:S(2)}) %collective-permute-start.1) | collective-permute-done | bytes 24608 | tf_op jit(solution)/shard_map/while/body/eval_jaxpr/ppermute | solution.py:17
  162.5 4.2 %collective-permute-done.3 = bf16[1,3,32,1,128]{4,2,3,1,0:T(8,128)(2,1)S(1)} collective-permute-done((bf16[1,3,32,1,128]{4,2,3,1,0:T(8,128)(2,1)S(1)}, bf16[1,3,32,1,128]{4,2,3,1,0:T(8,128)(2,1)S(1)}, u32[]{:S(2)}, u32[]{:S(2)}) %collective-permute-start.3) | collective-permute-done | bytes 24608 | tf_op jit(solution)/shard_map/while/body/eval_jaxpr/ppermute | solution.py:17
  172.5 11.0 %collective-permute-done.4 = f32[3,32,16,128]{3,1,2,0:T(8,128)} collective-permute-done((f32[3,32,16,128]{3,1,2,0:T(8,128)S(1)}, f32[3,32,16,128]{3,1,2,0:T(8,128)}, u32[]{:S(2)}, u32[]{:S(2)}) %collective-permute-start.4) | collective-permute-done | bytes 786464 | tf_op jit(solution)/shard_map/while/body/eval_jaxpr/ppermute | solution.py:28
  188.3 4.2 %collective-permute-done.1 = bf16[1,3,32,1,128]{4,2,3,1,0:T(8,128)(2,1)S(1)} collective-permute-done((bf16[1,3,32,1,128]{4,2,3,1,0:T(8,128)(2,1)S(1)}, bf16[1,3,32,1,128]{4,2,3,1,0:T(8,128)(2,1)S(1)}, u32[]{:S(2)}, u32[]{:S(2)}) %collective-permute-start.1) | collective-permute-done | bytes 24608 | tf_op jit(solution)/shard_map/while/body/eval_jaxpr/ppermute | solution.py:17
  198.5 4.2 %collective-permute-done.3 = bf16[1,3,32,1,128]{4,2,3,1,0:T(8,128)(2,1)S(1)} collective-permute-done((bf16[1,3,32,1,128]{4,2,3,1,0:T(8,128)(2,1)S(1)}, bf16[1,3,32,1,128]{4,2,3,1,0:T(8,128)(2,1)S(1)}, u32[]{:S(2)}, u32[]{:S(2)}) %collective-permute-start.3) | collective-permute-done | bytes 24608 | tf_op jit(solution)/shard_map/while/body/eval_jaxpr/ppermute | solution.py:17
  208.5 11.0 %collective-permute-done.4 = f32[3,32,16,128]{3,1,2,0:T(8,128)} collective-permute-done((f32[3,32,16,128]{3,1,2,0:T(8,128)S(1)}, f32[3,32,16,128]{3,1,2,0:T(8,128)}, u32[]{:S(2)}, u32[]{:S(2)}) %collective-permute-start.4) | collective-permute-done | bytes 786464 | tf_op jit(solution)/shard_map/while/body/eval_jaxpr/ppermute | solution.py:28
  224.3 4.2 %collective-permute-done.1 = bf16[1,3,32,1,128]{4,2,3,1,0:T(8,128)(2,1)S(1)} collective-permute-done((bf16[1,3,32,1,128]{4,2,3,1,0:T(8,128)(2,1)S(1)}, bf16[1,3,32,1,128]{4,2,3,1,0:T(8,128)(2,1)S(1)}, u32[]{:S(2)}, u32[]{:S(2)}) %collective-permute-start.1) | collective-permute-done | bytes 24608 | tf_op jit(solution)/shard_map/while/body/eval_jaxpr/ppermute | solution.py:17
  244.5 11.0 %collective-permute-done.4 = f32[3,32,16,128]{3,1,2,0:T(8,128)} collective-permute-done((f32[3,32,16,128]{3,1,2,0:T(8,128)S(1)}, f32[3,32,16,128]{3,1,2,0:T(8,128)}, u32[]{:S(2)}, u32[]{:S(2)}) %collective-permute-start.4) | collective-permute-done | bytes 786464 | tf_op jit(solution)/shard_map/while/body/eval_jaxpr/ppermute | solution.py:28
  280.5 11.0 %collective-permute-done.4 = f32[3,32,16,128]{3,1,2,0:T(8,128)} collective-permute-done((f32[3,32,16,128]{3,1,2,0:T(8,128)S(1)}, f32[3,32,16,128]{3,1,2,0:T(8,128)}, u32[]{:S(2)}, u32[]{:S(2)}) %collective-permute-start.4) | collective-permute-done | bytes 786464 | tf_op jit(solution)/shard_map/while/body/eval_jaxpr/ppermute | solution.py:28
  316.5 11.0 %collective-permute-done.4 = f32[3,32,16,128]{3,1,2,0:T(8,128)} collective-permute-done((f32[3,32,16,128]{3,1,2,0:T(8,128)S(1)}, f32[3,32,16,128]{3,1,2,0:T(8,128)}, u32[]{:S(2)}, u32[]{:S(2)}) %collective-permute-start.4) | collective-permute-done | bytes 786464 | tf_op jit(solution)/shard_map/while/body/eval_jaxpr/ppermute | solution.py:28
  352.5 11.0 %collective-permute-done.4 = f32[3,32,16,128]{3,1,2,0:T(8,128)} collective-permute-done((f32[3,32,16,128]{3,1,2,0:T(8,128)S(1)}, f32[3,32,16,128]{3,1,2,0:T(8,128)}, u32[]{:S(2)}, u32[]{:S(2)}) %collective-permute-start.4) | collective-permute-done | bytes 786464 | tf_op jit(solution)/shard_map/while/body/eval_jaxpr/ppermute | solution.py:28
  (381 shorter events, 204.3 us)
Async XLA Ops:
  1.9 14.3 %collective-permute-start.5 = (f32[3,32,16,128]{3,1,2,0:T(8,128)S(1)}, f32[3,32,16,128]{3,1,2,0:T(8,128)}, u32[]{:S(2)}, u32[]{:S(2)}) collective-permute-start(f32[3,32,16,128]{3,1,2,0:T(8,128)S(1)} %bitcast.180), channel_id=1, source_target_pairs={{0,4},{4,8},{8,12},{12,16},{16,20},{20,24},{24,28},{1,5},{5,9},{9,... | collective-permute-start | bytes 2359304 | tf_op jit(solution)/shard_map/ppermute | solution.py:28
  18.6 6.0 %collective-permute-start.6 = (bf16[2,3,32,1,128]{4,2,3,1,0:T(8,128)(2,1)S(1)}, bf16[2,3,32,1,128]{4,2,3,1,0:T(8,128)(2,1)S(1)}, u32[]{:S(2)}, u32[]{:S(2)}) collective-permute-start(bf16[2,3,32,1,128]{4,2,3,1,0:T(8,128)(2,1)S(1)} %get-tuple-element.135), channel_id=1, source_target_pairs={{0,1},{1,2},{2,3},{4,5},{5,6},{6,7},{8,9},{9,10},{10,11},{12,13},{... | collective-permute-start | bytes 147464 | tf_op jit(solution)/shard_map/ppermute | solution.py:17
  19.9 6.3 %collective-permute-start.7 = (bf16[2,3,32,1,128]{4,2,3,1,0:T(8,128)(2,1)S(1)}, bf16[2,3,32,1,128]{4,2,3,1,0:T(8,128)(2,1)S(1)}, u32[]{:S(2)}, u32[]{:S(2)}) collective-permute-start(bf16[2,3,32,1,128]{4,2,3,1,0:T(8,128)(2,1)S(1)} %get-tuple-element.136), channel_id=1, source_target_pairs={{1,0},{2,1},{3,2},{5,4},{6,5},{7,6},{9,8},{10,9},{11,10},{13,12},{... | collective-permute-start | bytes 147464 | tf_op jit(solution)/shard_map/ppermute | solution.py:20
  31.0 6.3 %collective-permute-start.8 = (bf16[2,3,32,1,128]{4,2,3,1,0:T(8,128)(2,1)S(1)}, bf16[2,3,32,1,128]{4,2,3,1,0:T(8,128)(2,1)S(1)}, u32[]{:S(2)}, u32[]{:S(2)}) collective-permute-start(bf16[2,3,32,1,128]{4,2,3,1,0:T(8,128)(2,1)S(1)} %get-tuple-element.133), channel_id=1, source_target_pairs={{0,1},{1,2},{2,3},{4,5},{5,6},{6,7},{8,9},{9,10},{10,11},{12,13},{... | collective-permute-start | bytes 147464 | tf_op jit(solution)/shard_map/ppermute | solution.py:17
  32.3 6.6 %collective-permute-start.9 = (bf16[2,3,32,1,128]{4,2,3,1,0:T(8,128)(2,1)S(1)}, bf16[2,3,32,1,128]{4,2,3,1,0:T(8,128)(2,1)S(1)}, u32[]{:S(2)}, u32[]{:S(2)}) collective-permute-start(bf16[2,3,32,1,128]{4,2,3,1,0:T(8,128)(2,1)S(1)} %get-tuple-element.134), channel_id=1, source_target_pairs={{1,0},{2,1},{3,2},{5,4},{6,5},{7,6},{9,8},{10,9},{11,10},{13,12},{... | collective-permute-start | bytes 147464 | tf_op jit(solution)/shard_map/ppermute | solution.py:20
  43.5 6.4 %collective-permute-start.10 = (bf16[2,3,32,1,128]{4,2,3,1,0:T(8,128)(2,1)S(1)}, bf16[2,3,32,1,128]{4,2,3,1,0:T(8,128)(2,1)S(1)}, u32[]{:S(2)}, u32[]{:S(2)}) collective-permute-start(bf16[2,3,32,1,128]{4,2,3,1,0:T(8,128)(2,1)S(1)} %get-tuple-element.131), channel_id=1, source_target_pairs={{0,1},{1,2},{2,3},{4,5},{5,6},{6,7},{8,9},{9,10},{10,11},{12,13},{... | collective-permute-start | bytes 147464 | tf_op jit(solution)/shard_map/ppermute | solution.py:17
  44.8 6.6 %collective-permute-start.11 = (bf16[2,3,32,1,128]{4,2,3,1,0:T(8,128)(2,1)S(1)}, bf16[2,3,32,1,128]{4,2,3,1,0:T(8,128)(2,1)S(1)}, u32[]{:S(2)}, u32[]{:S(2)}) collective-permute-start(bf16[2,3,32,1,128]{4,2,3,1,0:T(8,128)(2,1)S(1)} %get-tuple-element.132), channel_id=1, source_target_pairs={{1,0},{2,1},{3,2},{5,4},{6,5},{7,6},{9,8},{10,9},{11,10},{13,12},{... | collective-permute-start | bytes 147464 | tf_op jit(solution)/shard_map/ppermute | solution.py:20
  57.2 6.3 %collective-permute-start.12 = (bf16[2,3,32,1,128]{4,2,3,1,0:T(8,128)(2,1)S(1)}, bf16[2,3,32,1,128]{4,2,3,1,0:T(8,128)(2,1)S(1)}, u32[]{:S(2)}, u32[]{:S(2)}) collective-permute-start(bf16[2,3,32,1,128]{4,2,3,1,0:T(8,128)(2,1)S(1)} %get-tuple-element.129), channel_id=1, source_target_pairs={{0,1},{1,2},{2,3},{4,5},{5,6},{6,7},{8,9},{9,10},{10,11},{12,13},{... | collective-permute-start | bytes 147464 | tf_op jit(solution)/shard_map/ppermute | solution.py:17
  58.5 6.6 %collective-permute-start.13 = (bf16[2,3,32,1,128]{4,2,3,1,0:T(8,128)(2,1)S(1)}, bf16[2,3,32,1,128]{4,2,3,1,0:T(8,128)(2,1)S(1)}, u32[]{:S(2)}, u32[]{:S(2)}) collective-permute-start(bf16[2,3,32,1,128]{4,2,3,1,0:T(8,128)(2,1)S(1)} %get-tuple-element.130), channel_id=1, source_target_pairs={{1,0},{2,1},{3,2},{5,4},{6,5},{7,6},{9,8},{10,9},{11,10},{13,12},{... | collective-permute-start | bytes 147464 | tf_op jit(solution)/shard_map/ppermute | solution.py:20
  70.6 5.8 %collective-permute-start = (bf16[1,3,32,1,128]{4,2,3,1,0:T(8,128)(2,1)S(1)}, bf16[1,3,32,1,128]{4,2,3,1,0:T(8,128)(2,1)S(1)}, u32[]{:S(2)}, u32[]{:S(2)}) collective-permute-start(bf16[1,3,32,1,128]{4,2,3,1,0:T(8,128)(2,1)S(1)} %get-tuple-element.188), channel_id=1, source_target_pairs={{1,0},{2,1},{3,2},{5,4},{6,5},{7,6},{9,8},{10,9},{11,10},{13,12},{... | collective-permute-start | bytes 73736 | tf_op jit(solution)/shard_map/while/body/eval_jaxpr/ppermute | solution.py:20
  74.8 5.7 %collective-permute-start.1 = (bf16[1,3,32,1,128]{4,2,3,1,0:T(8,128)(2,1)S(1)}, bf16[1,3,32,1,128]{4,2,3,1,0:T(8,128)(2,1)S(1)}, u32[]{:S(2)}, u32[]{:S(2)}) collective-permute-start(bf16[1,3,32,1,128]{4,2,3,1,0:T(8,128)(2,1)S(1)} %get-tuple-element.189), channel_id=1, source_target_pairs={{0,1},{1,2},{2,3},{4,5},{5,6},{6,7},{8,9},{9,10},{10,11},{12,13},{... | collective-permute-start | bytes 73736 | tf_op jit(solution)/shard_map/while/body/eval_jaxpr/ppermute | solution.py:17
  87.0 5.7 %collective-permute-start.3 = (bf16[1,3,32,1,128]{4,2,3,1,0:T(8,128)(2,1)S(1)}, bf16[1,3,32,1,128]{4,2,3,1,0:T(8,128)(2,1)S(1)}, u32[]{:S(2)}, u32[]{:S(2)}) collective-permute-start(bf16[1,3,32,1,128]{4,2,3,1,0:T(8,128)(2,1)S(1)} %get-tuple-element.191), channel_id=1, source_target_pairs={{0,1},{1,2},{2,3},{4,5},{5,6},{6,7},{8,9},{9,10},{10,11},{12,13},{... | collective-permute-start | bytes 73736 | tf_op jit(solution)/shard_map/while/body/eval_jaxpr/ppermute | solution.py:17
  95.2 14.3 %collective-permute-start.4 = (f32[3,32,16,128]{3,1,2,0:T(8,128)S(1)}, f32[3,32,16,128]{3,1,2,0:T(8,128)}, u32[]{:S(2)}, u32[]{:S(2)}) collective-permute-start(f32[3,32,16,128]{3,1,2,0:T(8,128)S(1)} %fusion.95), channel_id=1, source_target_pairs={{0,4},{4,8},{8,12},{12,16},{16,20},{20,24},{24,28},{1,5},{5,9},{9,... | collective-permute-start | bytes 2359304 | tf_op jit(solution)/shard_map/while/body/eval_jaxpr/ppermute | solution.py:28
  114.8 5.7 %collective-permute-start.1 = (bf16[1,3,32,1,128]{4,2,3,1,0:T(8,128)(2,1)S(1)}, bf16[1,3,32,1,128]{4,2,3,1,0:T(8,128)(2,1)S(1)}, u32[]{:S(2)}, u32[]{:S(2)}) collective-permute-start(bf16[1,3,32,1,128]{4,2,3,1,0:T(8,128)(2,1)S(1)} %get-tuple-element.189), channel_id=1, source_target_pairs={{0,1},{1,2},{2,3},{4,5},{5,6},{6,7},{8,9},{9,10},{10,11},{12,13},{... | collective-permute-start | bytes 73736 | tf_op jit(solution)/shard_map/while/body/eval_jaxpr/ppermute | solution.py:17
  125.0 5.7 %collective-permute-start.3 = (bf16[1,3,32,1,128]{4,2,3,1,0:T(8,128)(2,1)S(1)}, bf16[1,3,32,1,128]{4,2,3,1,0:T(8,128)(2,1)S(1)}, u32[]{:S(2)}, u32[]{:S(2)}) collective-permute-start(bf16[1,3,32,1,128]{4,2,3,1,0:T(8,128)(2,1)S(1)} %get-tuple-element.191), channel_id=1, source_target_pairs={{0,1},{1,2},{2,3},{4,5},{5,6},{6,7},{8,9},{9,10},{10,11},{12,13},{... | collective-permute-start | bytes 73736 | tf_op jit(solution)/shard_map/while/body/eval_jaxpr/ppermute | solution.py:17
  133.2 14.3 %collective-permute-start.4 = (f32[3,32,16,128]{3,1,2,0:T(8,128)S(1)}, f32[3,32,16,128]{3,1,2,0:T(8,128)}, u32[]{:S(2)}, u32[]{:S(2)}) collective-permute-start(f32[3,32,16,128]{3,1,2,0:T(8,128)S(1)} %fusion.95), channel_id=1, source_target_pairs={{0,4},{4,8},{8,12},{12,16},{16,20},{20,24},{24,28},{1,5},{5,9},{9,... | collective-permute-start | bytes 2359304 | tf_op jit(solution)/shard_map/while/body/eval_jaxpr/ppermute | solution.py:28
  150.8 5.7 %collective-permute-start.1 = (bf16[1,3,32,1,128]{4,2,3,1,0:T(8,128)(2,1)S(1)}, bf16[1,3,32,1,128]{4,2,3,1,0:T(8,128)(2,1)S(1)}, u32[]{:S(2)}, u32[]{:S(2)}) collective-permute-start(bf16[1,3,32,1,128]{4,2,3,1,0:T(8,128)(2,1)S(1)} %get-tuple-element.189), channel_id=1, source_target_pairs={{0,1},{1,2},{2,3},{4,5},{5,6},{6,7},{8,9},{9,10},{10,11},{12,13},{... | collective-permute-start | bytes 73736 | tf_op jit(solution)/shard_map/while/body/eval_jaxpr/ppermute | solution.py:17
  161.0 5.7 %collective-permute-start.3 = (bf16[1,3,32,1,128]{4,2,3,1,0:T(8,128)(2,1)S(1)}, bf16[1,3,32,1,128]{4,2,3,1,0:T(8,128)(2,1)S(1)}, u32[]{:S(2)}, u32[]{:S(2)}) collective-permute-start(bf16[1,3,32,1,128]{4,2,3,1,0:T(8,128)(2,1)S(1)} %get-tuple-element.191), channel_id=1, source_target_pairs={{0,1},{1,2},{2,3},{4,5},{5,6},{6,7},{8,9},{9,10},{10,11},{12,13},{... | collective-permute-start | bytes 73736 | tf_op jit(solution)/shard_map/while/body/eval_jaxpr/ppermute | solution.py:17
  169.2 14.3 %collective-permute-start.4 = (f32[3,32,16,128]{3,1,2,0:T(8,128)S(1)}, f32[3,32,16,128]{3,1,2,0:T(8,128)}, u32[]{:S(2)}, u32[]{:S(2)}) collective-permute-start(f32[3,32,16,128]{3,1,2,0:T(8,128)S(1)} %fusion.95), channel_id=1, source_target_pairs={{0,4},{4,8},{8,12},{12,16},{16,20},{20,24},{24,28},{1,5},{5,9},{9,... | collective-permute-start | bytes 2359304 | tf_op jit(solution)/shard_map/while/body/eval_jaxpr/ppermute | solution.py:28
  205.2 14.3 %collective-permute-start.4 = (f32[3,32,16,128]{3,1,2,0:T(8,128)S(1)}, f32[3,32,16,128]{3,1,2,0:T(8,128)}, u32[]{:S(2)}, u32[]{:S(2)}) collective-permute-start(f32[3,32,16,128]{3,1,2,0:T(8,128)S(1)} %fusion.95), channel_id=1, source_target_pairs={{0,4},{4,8},{8,12},{12,16},{16,20},{20,24},{24,28},{1,5},{5,9},{9,... | collective-permute-start | bytes 2359304 | tf_op jit(solution)/shard_map/while/body/eval_jaxpr/ppermute | solution.py:28
  241.2 14.3 %collective-permute-start.4 = (f32[3,32,16,128]{3,1,2,0:T(8,128)S(1)}, f32[3,32,16,128]{3,1,2,0:T(8,128)}, u32[]{:S(2)}, u32[]{:S(2)}) collective-permute-start(f32[3,32,16,128]{3,1,2,0:T(8,128)S(1)} %fusion.95), channel_id=1, source_target_pairs={{0,4},{4,8},{8,12},{12,16},{16,20},{20,24},{24,28},{1,5},{5,9},{9,... | collective-permute-start | bytes 2359304 | tf_op jit(solution)/shard_map/while/body/eval_jaxpr/ppermute | solution.py:28
  277.2 14.3 %collective-permute-start.4 = (f32[3,32,16,128]{3,1,2,0:T(8,128)S(1)}, f32[3,32,16,128]{3,1,2,0:T(8,128)}, u32[]{:S(2)}, u32[]{:S(2)}) collective-permute-start(f32[3,32,16,128]{3,1,2,0:T(8,128)S(1)} %fusion.95), channel_id=1, source_target_pairs={{0,4},{4,8},{8,12},{12,16},{16,20},{20,24},{24,28},{1,5},{5,9},{9,... | collective-permute-start | bytes 2359304 | tf_op jit(solution)/shard_map/while/body/eval_jaxpr/ppermute | solution.py:28
  313.2 14.3 %collective-permute-start.4 = (f32[3,32,16,128]{3,1,2,0:T(8,128)S(1)}, f32[3,32,16,128]{3,1,2,0:T(8,128)}, u32[]{:S(2)}, u32[]{:S(2)}) collective-permute-start(f32[3,32,16,128]{3,1,2,0:T(8,128)S(1)} %fusion.95), channel_id=1, source_target_pairs={{0,4},{4,8},{8,12},{12,16},{16,20},{20,24},{24,28},{1,5},{5,9},{9,... | collective-permute-start | bytes 2359304 | tf_op jit(solution)/shard_map/while/body/eval_jaxpr/ppermute | solution.py:28
  349.2 14.3 %collective-permute-start.4 = (f32[3,32,16,128]{3,1,2,0:T(8,128)S(1)}, f32[3,32,16,128]{3,1,2,0:T(8,128)}, u32[]{:S(2)}, u32[]{:S(2)}) collective-permute-start(f32[3,32,16,128]{3,1,2,0:T(8,128)S(1)} %fusion.95), channel_id=1, source_target_pairs={{0,4},{4,8},{8,12},{12,16},{16,20},{20,24},{24,28},{1,5},{5,9},{9,... | collective-permute-start | bytes 2359304 | tf_op jit(solution)/shard_map/while/body/eval_jaxpr/ppermute | solution.py:28
  (38 other events, 243.5 us)
where the time goes:
time: 370 us; the launch traced here: 368 us
  waiting for transfers between devices  178 us (48%)
  starting transfers between devices  99.5 us (27%)
  other arithmetic  39.6 us (11%)
  local copies, waits for them, and re-layouts  29.6 us (8%)
  matrix products  19.8 us (5%)
    ppermute x9, waiting for transfers between devices, passed_along(): return lax.ppermute(value, axis, pairs)  100 us
    ppermute x20, waiting for transfers between devices, extended_2(): lax.ppermute(lax.slice_in_dim(block, block.shape[dim] - width, None, axis...  67.9 us
    ppermute x20, starting transfers between devices, extended_2(): lax.ppermute(lax.slice_in_dim(block, 0, width, axis=dim), axis, backward)  56.3 us
    ppermute x20, starting transfers between devices, extended_2(): lax.ppermute(lax.slice_in_dim(block, block.shape[dim] - width, None, axis...  25.8 us
    dot_general x20, matrix products, convolve(): jnp.einsum('iok,inkrw->inorw', matrices, patches, preferred_element_type=...  19.8 us
    ppermute x9, starting transfers between devices, passed_along(): return lax.ppermute(value, axis, pairs)  17.3 us
    while x96, local copies, waits for them, and re-layouts  11.8 us
    another operation x8, other arithmetic, advance(): return jnp.stack(results)  10.9 us
  transfers between devices with their start and end apart: 49, of which 48 were waited for; matrix products, arithmetic and copies ran while one was open for 3% of the time, Pallas kernels for 0%

commit v1 on v0

v1 whole, which is shorter than its diff:
```python
import functools

import jax
import jax.numpy as jnp
from jax import lax
from jax.experimental import pallas as pl
from jax.experimental.pallas import tpu as pltpu
from jax.sharding import PartitionSpec as P

M = 4
LEVELS = 2
STEP = 0.125
GROUP = 6
MESH = pl.DeviceIdType.MESH
F32 = jnp.float32
BF16 = jnp.bfloat16


def groups(low, high):
    found = []
    start = low
    while start < high:
        first = min(start, high - GROUP)
        found.append((first, start - first))
        start += GROUP
    return found


def chunks(low, high):
    return [(start, min(start + GROUP, high)) for start in range(low, high, GROUP)]


def put(patches, start, value):
    count, channels, breadth = value.shape
    flat = value.reshape(count * channels, breadth)
    column = lax.broadcasted_iota(jnp.int32, flat.shape, 1)
    left = jnp.where(column == 0, 0.0, pltpu.roll(flat, 1, 1))
    right = jnp.where(column == breadth - 1, 0.0, pltpu.roll(flat, breadth - 1, 1))
    rows = pl.ds(start, count)
    for place, part in enumerate((left, flat, right)):
        patches[rows, place * channels : (place + 1) * channels, :] = part.reshape(value.shape).astype(BF16)


def conv(matrix_ref, layer, patches, start, skip):
    window = patches[start - 1 : start + GROUP + 1]
    channels = window.shape[1] // 3
    flat = window.reshape(window.shape[0] * window.shape[1], window.shape[2])
    product = jnp.dot(matrix_ref[layer, skip * channels :, :], flat, preferred_element_type=F32)
    return product.reshape(GROUP - skip, channels, window.shape[2])


def masked(value, low, first, last, above, below):
    high = low + value.shape[0]
    parts = []
    if low < first:
        parts.append(value[: min(first, high) - low] * above)
    if max(low, first) < min(high, last):
        parts.append(value[max(low, first) - low : min(high, last) - low])
    if high > last:
        parts.append(value[max(low, last) - low :] * below)
    return parts[0] if len(parts) == 1 else jnp.concatenate(parts, axis=0)


def cycle_kernel(
    sections, bands, matrix, guess, image, out,
    wide0, wide1, entry, leave, state0, state1, patch0, patch1, defect0, defect1,
    start_send, start_recv, chain_send, chain_recv,
):
    batch, height = image.shape[0], image.shape[1]
    s = lax.axis_index("layer")
    r = lax.axis_index("rows")
    above = jnp.where(r > 0, 1.0, 0.0).astype(F32)
    below = jnp.where(r < bands - 1, 1.0, 0.0).astype(F32)
    deep0, deep1, near = M + 1, M, LEVELS

    has = {
        (i, j): functools.reduce(
            jnp.logical_and,
            [c for c in (
                s > 0 if i < 0 else (s < sections - 1 if i > 0 else None),
                r > 0 if j < 0 else (r < bands - 1 if j > 0 else None),
            ) if c is not None],
        )
        for i in (-1, 0, 1) for j in (-1, 0, 1) if (i, j) != (0, 0)
    }

    barrier = pltpu.get_barrier_semaphore()
    total = 0
    for (i, j), there in has.items():
        @pl.when(there)
        def _(i=i, j=j):
            pl.semaphore_signal(barrier, inc=1, device_id=(s + i, r + j), device_id_type=MESH)
        total = total + there.astype(jnp.int32)
    pl.semaphore_wait(barrier, total)

    def start_copy(source, target, slot, img, i, j):
        return pltpu.make_async_remote_copy(
            src_ref=source, dst_ref=target,
            send_sem=start_send.at[slot, img], recv_sem=start_recv.at[slot, img],
            device_id=(s + i, r + j), device_id_type=MESH,
        )

    def band0(img):
        return start_copy(guess.at[1, img], wide0.at[img, pl.ds(deep0, height)], 0, img, 1, 0)

    def down0(img, own):
        source = image.at[img] if own else guess.at[1, img]
        return start_copy(
            source.at[pl.ds(height - deep0, deep0)], wide0.at[img, pl.ds(0, deep0)],
            5 if own else 1, img, 0 if own else 1, 1)

    def up0(img, own):
        source = image.at[img] if own else guess.at[1, img]
        return start_copy(
            source.at[pl.ds(0, deep0)], wide0.at[img, pl.ds(deep0 + height, deep0)],
            6 if own else 2, img, 0 if own else 1, -1)

    def down1(img):
        return start_copy(
            guess.at[0, img, pl.ds(height - deep1, deep1)], wide1.at[img, pl.ds(0, deep1)], 3, img, 0, 1)

    def up1(img):
        return start_copy(
            guess.at[0, img, pl.ds(0, deep1)], wide1.at[img, pl.ds(deep1 + height, deep1)], 4, img, 0, -1)

    first = s == 0
    plan = [
        (band0, s < sections - 1, s > 0),
        (functools.partial(down0, own=True), first & (r < bands - 1), first & (r > 0)),
        (functools.partial(up0, own=True), first & (r > 0), first & (r < bands - 1)),
        (functools.partial(down0, own=False), has[1, 1], has[-1, -1]),
        (functools.partial(up0, own=False), has[1, -1], has[-1, 1]),
        (down1, r < bands - 1, r > 0),
        (up1, r > 0, r < bands - 1),
    ]
    for img in range(batch):
        for copy, sends, _ in plan:
            @pl.when(sends)
            def _(img=img, copy=copy):
                copy(img).start()

    @pl.when(r == 0)
    def _():
        for img in range(batch):
            wide0[img, :deep0] = jnp.zeros((deep0,) + wide0.shape[2:], BF16)
            wide1[img, :deep1] = jnp.zeros((deep1,) + wide1.shape[2:], BF16)
            entry[img, :near] = jnp.zeros((near,) + entry.shape[2:], BF16)

    @pl.when(r == bands - 1)
    def _():
        for img in range(batch):
            wide0[img, deep0 + height :] = jnp.zeros((deep0,) + wide0.shape[2:], BF16)
            wide1[img, deep1 + height :] = jnp.zeros((deep1,) + wide1.shape[2:], BF16)
            entry[img, near + height :] = jnp.zeros((near,) + entry.shape[2:], BF16)

    for img in range(batch):
        wide1[img, deep1 : deep1 + height] = guess[0, img]

    @pl.when(first)
    def _():
        for img in range(batch):
            wide0[img, deep0 : deep0 + height] = image[img]

    def relax(img):
        for copy, _, receives in plan:
            @pl.when(receives)
            def _(copy=copy):
                copy(img).wait_recv()
        anchors = (
            (1, wide1, deep1, state1, patch1, defect1, 0),
            (0, wide0, deep0, state0, patch0, defect0, 1),
        )
        for _, wide, deep, state, patch, _, _ in anchors:
            for low, high in chunks(0, height + 2 * deep):
                value = wide[img, low:high].astype(F32)
                state[low:high] = value
                put(patch.at[0], low, value)
        for j in range(M):
            for point, _, deep, state, patch, defect, extra in anchors:
                end = deep + height
                for start, skip in groups(j + 1, end + deep - j - 1):
                    low, high = start + skip, start + GROUP
                    change = STEP * jnp.tanh(conv(matrix, point * M + j, patch.at[j % 2], start, skip))
                    old = state[low:high]
                    new = old + change
                    a, b = max(low, deep - extra), min(high, end + extra)
                    if a < b:
                        rows = pl.ds(a - deep + extra, b - a)
                        part = slice(a - low, b - low)
                        if j == 0:
                            defect[img, rows] = -(old + M * change)[part]
                        if j == M - 1:
                            defect[img, rows] = defect[img, rows] + new[part]
                    if j < M - 1:
                        new = masked(new, low, deep, end, above, below)
                        state[low:high] = new
                        put(patch.at[(j + 1) % 2], low, new)

    def chain_copy(source, target, slot, img, j):
        return pltpu.make_async_remote_copy(
            src_ref=leave.at[img, source], dst_ref=entry.at[img, target],
            send_sem=chain_send.at[slot, img], recv_sem=chain_recv.at[slot, img],
            device_id=(s + 1, r + j), device_id_type=MESH,
        )

    def hand_on(img):
        return (
            (chain_copy(pl.ds(height - near, near), pl.ds(0, near), 0, img, 1), has[1, 1], has[-1, -1]),
            (chain_copy(pl.ds(0, near), pl.ds(near + height, near), 1, img, -1), has[1, -1], has[-1, 1]),
            (chain_copy(pl.ds(0, height), pl.ds(near, height), 2, img, 0), has[1, 0], has[-1, 0]),
        )

    def coarse(img):
        for copy, _, receives in hand_on(img):
            @pl.when(receives)
            def _(copy=copy):
                copy.wait_recv()

        @pl.when(first)
        def _():
            entry[img] = wide0[img, deep0 - near : deep0 + height + near]

        end = near + height
        for low, high in chunks(0, end + near):
            value = entry[img, low:high].astype(F32)
            state0[low:high] = value
            put(patch0.at[0], low, value)
        for start, skip in groups(1, end + 1):
            low, high = start + skip, start + GROUP
            change = (M * STEP) * jnp.tanh(conv(matrix, 0, patch0.at[0], start, skip))
            new = (state0[low:high] + change) + defect0[img, low - 1 : high - 1]
            new = masked(new, low, near, end, above, below)
            state0[low:high] = new
            put(patch0.at[1], low, new)
            a, b = max(low, near), min(high, end)
            out[0, img, a - near : b - near] = new[a - low : b - low]
        for start, skip in groups(near, end):
            low, high = start + skip, start + GROUP
            change = (M * STEP) * jnp.tanh(conv(matrix, M, patch0.at[1], start, skip))
            rows = slice(low - near, high - near)
            new = (state0[low:high] + change) + defect1[img, rows]
            out[1, img, rows] = new
            leave[img, rows] = new.astype(BF16)
        for copy, sends, _ in hand_on(img):
            @pl.when(sends)
            def _(copy=copy):
                copy.start()

    def tick(t, carry):
        relaxes = jnp.where(first, t % 2 == 0, t < batch)
        img = jnp.where(first, t // 2, t % batch)

        @pl.when(relaxes)
        def _():
            relax(img)

        @pl.when(jnp.logical_not(relaxes))
        def _():
            coarse(img)

        return carry

    lax.fori_loop(0, 2 * batch, tick, 0)

    for img in range(batch):
        for copy, sends, _ in plan:
            @pl.when(sends)
            def _(img=img, copy=copy):
                copy(img).wait_send()
        for copy, sends, _ in hand_on(img):
            @pl.when(sends)
            def _(copy=copy):
                copy.wait_send()


def toeplitz(weights):
    tap = weights.shape[2] // 3
    return jnp.concatenate(
        [
            jnp.pad(weights, ((0, 0), (0, 0), (row * tap, (GROUP - 1 - row) * tap)))
            for row in range(GROUP)
        ],
        axis=1,
    )


def per_device(sections, bands, weights, image, guess):
    levels, batch, channels, height, breadth = guess.shape
    matrix = toeplitz(weights)
    moved = jnp.transpose(guess, (0, 1, 3, 2, 4)).astype(BF16)
    picture = jnp.transpose(image, (0, 2, 1, 3)).astype(BF16)
    rows0, rows1 = height + 2 * (M + 1), height + 2 * M
    plane = (channels, breadth)
    wide_plane = (3 * channels, breadth)
    result = pl.pallas_call(
        functools.partial(cycle_kernel, sections, bands),
        out_shape=jax.ShapeDtypeStruct((levels, batch, height) + plane, F32),
        in_specs=[pl.BlockSpec(memory_space=pltpu.VMEM)] * 3,
        out_specs=pl.BlockSpec(memory_space=pltpu.VMEM),
        scratch_shapes=[
            pltpu.VMEM((batch, rows0) + plane, BF16),
            pltpu.VMEM((batch, rows1) + plane, BF16),
            pltpu.VMEM((batch, height + 2 * LEVELS) + plane, BF16),
            pltpu.VMEM((batch, height) + plane, BF16),
            pltpu.VMEM((rows0,) + plane, F32),
            pltpu.VMEM((rows1,) + plane, F32),
            pltpu.VMEM((2, rows0) + wide_plane, BF16),
            pltpu.VMEM((2, rows1) + wide_plane, BF16),
            pltpu.VMEM((batch, height + 2) + plane, F32),
            pltpu.VMEM((batch, height) + plane, F32),
            pltpu.SemaphoreType.DMA((7, batch)),
            pltpu.SemaphoreType.DMA((7, batch)),
            pltpu.SemaphoreType.DMA((3, batch)),
            pltpu.SemaphoreType.DMA((3, batch)),
        ],
        compiler_params=pltpu.CompilerParams(
            collective_id=0, has_side_effects=True, vmem_limit_bytes=40 * 1024 * 1024
        ),
        cost_estimate=pl.CostEstimate(
            flops=2_000_000_000, bytes_accessed=8_000_000, transcendentals=2_500_000
        ),
    )(matrix, moved, picture)
    return jnp.transpose(result, (0, 1, 3, 2, 4))


def solution(mesh):
    sizes = dict(mesh.shape)
    return jax.shard_map(
        functools.partial(per_device, sizes["layer"], sizes["rows"]),
        mesh=mesh,
        in_specs=(
            P("layer", None, None),
            P(None, None, "rows", None),
            P("layer", None, None, "rows", None),
        ),
        out_specs=P("layer", None, None, "rows", None),
        check_vma=False,
    )
```

time: 370 us -> 51.4 us (0.14)
  the two profiles are of different devices: /device:TPU:28 before, /device:TPU:7 now
where the time goes in v1:
time: 51.4 us; the launch traced here: 51.2 us
  Pallas kernels  43.8 us (85%)
  local copies, waits for them, and re-layouts  7.33 us (14%)
    pallas_call x1, Pallas kernels, per_device(): pl.pallas_call(functools.partial(cycle_kernel, sections, bands), out_shap...  43.8 us
    unnamed x13, local copies, waits for them, and re-layouts  5.16 us
    transpose x1, local copies, waits for them, and re-layouts, per_device(): return jnp.transpose(result, (0, 1, 3, 2, 4))  2.05 us

profile of v1, /device:TPU:7, one launch (start us, length us, event | category | flops | bytes accessed | tf_op | source)
XLA Modules:
  0.0 51.2 jit_solution(425035140390791421)
XLA Ops:
  0.0 0.0 copy-start
  0.0 0.0 copy-start.1
  0.0 1.1 %pad_dynamic-update-slice_fusion.5 = bf16[8,192,768]{2,1,0:T(8,128)(2,1)S(1)} fusion(bf16[8,32,288]{2,1,0:T(8,128)(2,1)} %param.3), kind=kLoop, calls=%fused_computation.9 | loop fusion | bytes 540672
  1.1 1.1 %pad_dynamic-update-slice_fusion.4 = bf16[8,192,768]{2,1,0:T(8,128)(2,1)S(1)} fusion(bf16[8,192,768]{2,1,0:T(8,128)(2,1)S(1)} %pad_dynamic-update-slice_fusion.5, bf16[8,32,288]{2,1,0:T(8,128)(2,1)} %param.3), kind=kLoop, calls=%fused_computation.8 | loop fusion | bytes 540672
  2.2 0.0 copy-start.2
  2.2 1.1 %pad_dynamic-update-slice_fusion.3 = bf16[8,192,768]{2,1,0:T(8,128)(2,1)S(1)} fusion(bf16[8,192,768]{2,1,0:T(8,128)(2,1)S(1)} %pad_dynamic-update-slice_fusion.4, bf16[8,32,288]{2,1,0:T(8,128)(2,1)} %param.3), kind=kLoop, calls=%fused_computation.7 | loop fusion | bytes 540672
  3.3 1.1 %pad_dynamic-update-slice_fusion.2 = bf16[8,192,768]{2,1,0:T(8,128)(2,1)S(1)} fusion(bf16[8,192,768]{2,1,0:T(8,128)(2,1)S(1)} %pad_dynamic-update-slice_fusion.3, bf16[8,32,288]{2,1,0:T(8,128)(2,1)} %param.3), kind=kLoop, calls=%fused_computation.6 | loop fusion | bytes 540672
  4.4 0.0 copy-done
  4.4 0.1 pad_dynamic-update-slice_fusion.matrix
  4.6 0.0 copy-done.1
  4.6 0.5 copy.13
  5.1 0.0 copy-done.2
  5.1 0.3 copy.14
  5.4 43.8 %shard_map.37 = f32[2,3,16,32,128]{4,3,2,1,0:T(8,128)S(1)} custom-call(bf16[8,192,768]{2,1,0:T(8,128)(2,1)S(1)} %pad_dynamic-update-slice_fusion.matrix, bf16[2,3,16,32,128]{4,3,2,1,0:T(8,128)(2,1)S(1)} %bitcast.8, bf16[3,16,32,128]{3,2,1,0:T(8,128)(2,1)S(1)} %bitcast.9), custom_call_target="tpu_custom_call" | custom-call | flops 2000000000 | bytes 8000000 | tf_op jit(solution)/shard_map/pallas_call | solution.py:295
  49.1 2.0 %copy.6 = f32[2,3,32,16,128]{4,3,2,1,0:T(8,128)} copy(f32[2,3,32,16,128]{4,2,3,1,0:T(8,128)S(1)} %bitcast.7) | data formatting | bytes 3145728 | tf_op jit(solution)/shard_map/transpose | solution.py:323
  (1 shorter events, 0.0 us)
Async XLA Ops:
  0.0 4.4 %copy-start = (bf16[8,32,288]{2,1,0:T(8,128)(2,1)S(1)}, bf16[8,32,288]{2,1,0:T(8,128)(2,1)}, u32[]{:S(2)}) copy-start(bf16[8,32,288]{2,1,0:T(8,128)(2,1)} %param.3) | copy-start | bytes 442372
  0.0 4.6 %copy-start.1 = (f32[2,3,32,16,128]{4,3,2,1,0:T(8,128)S(1)}, f32[2,3,32,16,128]{4,3,2,1,0:T(8,128)}, u32[]{:S(2)}) copy-start(f32[2,3,32,16,128]{4,3,2,1,0:T(8,128)} %param.5) | copy-start | bytes 4718596
  2.2 2.9 %copy-start.2 = (f32[3,32,16,128]{3,2,1,0:T(8,128)S(1)}, f32[3,32,16,128]{3,2,1,0:T(8,128)}, u32[]{:S(2)}) copy-start(f32[3,32,16,128]{3,2,1,0:T(8,128)} %param.4) | copy-start | bytes 2359300

commit v2 on v1

--- a/solution.py
+++ b/solution.py
@@ -16,14 +16,12 @@
 BF16 = jnp.bfloat16
 
 
-def groups(low, high):
-    found = []
-    start = low
-    while start < high:
-        first = min(start, high - GROUP)
-        found.append((first, start - first))
-        start += GROUP
-    return found
+def pairs(low, high):
+    count = high - low
+    upper = -(-count // 4)
+    lower = count // 2 - upper
+    middle = low + 2 * upper
+    return [(low, upper, low - 1, 0), (middle, lower, middle - 1 - (GROUP - lower), GROUP - lower)]
 
 
 def chunks(low, high):
@@ -41,12 +39,18 @@
         patches[rows, place * channels : (place + 1) * channels, :] = part.reshape(value.shape).astype(BF16)
 
 
-def conv(matrix_ref, layer, patches, start, skip):
-    window = patches[start - 1 : start + GROUP + 1]
-    channels = window.shape[1] // 3
-    flat = window.reshape(window.shape[0] * window.shape[1], window.shape[2])
-    product = jnp.dot(matrix_ref[layer, skip * channels :, :], flat, preferred_element_type=F32)
-    return product.reshape(GROUP - skip, channels, window.shape[2])
+def conv(matrix_ref, layer, patches, size, window, skip):
+    depth, width, breadth = patches.shape
+    channels = width // 3
+    parts = [
+        patches[window + k * size : window + k * size + GROUP + 2].reshape((GROUP + 2) * width, breadth)
+        for k in range(2)
+    ]
+    rows = matrix_ref[layer, skip * channels : (skip + size) * channels, :]
+    product = jnp.dot(rows, jnp.concatenate(parts, axis=1), preferred_element_type=F32)
+    return [
+        product[:, k * breadth : (k + 1) * breadth].reshape(size, channels, breadth) for k in range(2)
+    ]
 
 
 def masked(value, low, first, last, above, below):
@@ -62,8 +66,8 @@
 
 
 def cycle_kernel(
-    sections, bands, matrix, guess, image, out,
-    wide0, wide1, entry, leave, state0, state1, patch0, patch1, defect0, defect1,
+    sections, bands, narrow, guess, image, out,
+    matrix, wide0, wide1, entry, leave, state0, state1, patch0, patch1, defect0, defect1,
     start_send, start_recv, chain_send, chain_recv,
 ):
     batch, height = image.shape[0], image.shape[1]
@@ -161,6 +165,18 @@
         for img in range(batch):
             wide0[img, deep0 : deep0 + height] = image[img]
 
+    channels = narrow.shape[1]
+    for layer in range(narrow.shape[0]):
+        taps = narrow[layer].astype(F32)
+        for k in range(GROUP):
+            moved = taps if k == 0 else pltpu.roll(taps, k * 3 * channels, 1)
+            matrix[layer, k * channels : (k + 1) * channels, :] = moved.astype(BF16)
+
+    def convolved(layer, patches, low, high):
+        for first_row, size, window, skip in pairs(low, high):
+            for k, product in enumerate(conv(matrix, layer, patches, size, window, skip)):
+                yield first_row + k * size, first_row + (k + 1) * size, product
+
     def relax(img):
         for copy, _, receives in plan:
             @pl.when(receives)
@@ -178,9 +194,8 @@
         for j in range(M):
             for point, _, deep, state, patch, defect, extra in anchors:
                 end = deep + height
-                for start, skip in groups(j + 1, end + deep - j - 1):
-                    low, high = start + skip, start + GROUP
-                    change = STEP * jnp.tanh(conv(matrix, point * M + j, patch.at[j % 2], start, skip))
+                for low, high, product in convolved(point * M + j, patch.at[j % 2], j + 1, end + deep - j - 1):
+                    change = STEP * jnp.tanh(product)
                     old = state[low:high]
                     new = old + change
                     a, b = max(low, deep - extra), min(high, end + extra)
@@ -204,14 +219,17 @@
         )
 
     def hand_on(img):
+        half = height // 2
         return (
-            (chain_copy(pl.ds(height - near, near), pl.ds(0, near), 0, img, 1), has[1, 1], has[-1, -1]),
-            (chain_copy(pl.ds(0, near), pl.ds(near + height, near), 1, img, -1), has[1, -1], has[-1, 1]),
-            (chain_copy(pl.ds(0, height), pl.ds(near, height), 2, img, 0), has[1, 0], has[-1, 0]),
+            (chain_copy(pl.ds(0, near), pl.ds(near + height, near), 0, img, -1), has[1, -1], has[-1, 1], near),
+            (chain_copy(pl.ds(0, half), pl.ds(near, half), 1, img, 0), has[1, 0], has[-1, 0], half),
+            (chain_copy(pl.ds(height - near, near), pl.ds(0, near), 2, img, 1), has[1, 1], has[-1, -1], height),
+            (chain_copy(pl.ds(half, height - half), pl.ds(near + half, height - half), 3, img, 0),
+             has[1, 0], has[-1, 0], height),
         )
 
     def coarse(img):
-        for copy, _, receives in hand_on(img):
+        for copy, _, receives, _ in hand_on(img):
             @pl.when(receives)
             def _(copy=copy):
                 copy.wait_recv()
@@ -225,26 +243,27 @@
             value = entry[img, low:high].astype(F32)
             state0[low:high] = value
             put(patch0.at[0], low, value)
-        for start, skip in groups(1, end + 1):
-            low, high = start + skip, start + GROUP
-            change = (M * STEP) * jnp.tanh(conv(matrix, 0, patch0.at[0], start, skip))
+        for low, high, product in convolved(0, patch0.at[0], 1, end + 1):
+            change = (M * STEP) * jnp.tanh(product)
             new = (state0[low:high] + change) + defect0[img, low - 1 : high - 1]
             new = masked(new, low, near, end, above, below)
             state0[low:high] = new
             put(patch0.at[1], low, new)
             a, b = max(low, near), min(high, end)
             out[0, img, a - near : b - near] = new[a - low : b - low]
-        for start, skip in groups(near, end):
-            low, high = start + skip, start + GROUP
-            change = (M * STEP) * jnp.tanh(conv(matrix, M, patch0.at[1], start, skip))
+        ready = list(hand_on(img))
+        for low, high, product in convolved(M, patch0.at[1], near, end):
+            change = (M * STEP) * jnp.tanh(product)
             rows = slice(low - near, high - near)
             new = (state0[low:high] + change) + defect1[img, rows]
             out[1, img, rows] = new
             leave[img, rows] = new.astype(BF16)
-        for copy, sends, _ in hand_on(img):
-            @pl.when(sends)
-            def _(copy=copy):
-                copy.start()
+            while ready and ready[0][3] <= high - near:
+                copy, sends, _, _ = ready.pop(0)
+
+                @pl.when(sends)
+                def _(copy=copy):
+                    copy.start()
 
     def tick(t, carry):
         relaxes = jnp.where(first, t % 2 == 0, t < batch)
@@ -267,26 +286,16 @@
             @pl.when(sends)
             def _(img=img, copy=copy):
                 copy(img).wait_send()
-        for copy, sends, _ in hand_on(img):
+        for copy, sends, _, _ in hand_on(img):
             @pl.when(sends)
             def _(copy=copy):
                 copy.wait_send()
 
 
-def toeplitz(weights):
-    tap = weights.shape[2] // 3
-    return jnp.concatenate(
-        [
-            jnp.pad(weights, ((0, 0), (0, 0), (row * tap, (GROUP - 1 - row) * tap)))
-            for row in range(GROUP)
-        ],
-        axis=1,
-    )
-
-
 def per_device(sections, bands, weights, image, guess):
     levels, batch, channels, height, breadth = guess.shape
-    matrix = toeplitz(weights)
+    window = (GROUP + 2) * 3 * channels
+    narrow = jnp.pad(weights, ((0, 0), (0, 0), (0, window - weights.shape[2])))
     moved = jnp.transpose(guess, (0, 1, 3, 2, 4)).astype(BF16)
     picture = jnp.transpose(image, (0, 2, 1, 3)).astype(BF16)
     rows0, rows1 = height + 2 * (M + 1), height + 2 * M
@@ -298,6 +307,7 @@
         in_specs=[pl.BlockSpec(memory_space=pltpu.VMEM)] * 3,
         out_specs=pl.BlockSpec(memory_space=pltpu.VMEM),
         scratch_shapes=[
+            pltpu.VMEM((weights.shape[0], GROUP * channels, window), BF16),
             pltpu.VMEM((batch, rows0) + plane, BF16),
             pltpu.VMEM((batch, rows1) + plane, BF16),
             pltpu.VMEM((batch, height + 2 * LEVELS) + plane, BF16),
@@ -310,8 +320,8 @@
             pltpu.VMEM((batch, height) + plane, F32),
             pltpu.SemaphoreType.DMA((7, batch)),
             pltpu.SemaphoreType.DMA((7, batch)),
-            pltpu.SemaphoreType.DMA((3, batch)),
-            pltpu.SemaphoreType.DMA((3, batch)),
+            pltpu.SemaphoreType.DMA((4, batch)),
+            pltpu.SemaphoreType.DMA((4, batch)),
         ],
         compiler_params=pltpu.CompilerParams(
             collective_id=0, has_side_effects=True, vmem_limit_bytes=40 * 1024 * 1024
@@ -319,7 +329,7 @@
         cost_estimate=pl.CostEstimate(
             flops=2_000_000_000, bytes_accessed=8_000_000, transcendentals=2_500_000
         ),
-    )(matrix, moved, picture)
+    )(narrow, moved, picture)
     return jnp.transpose(result, (0, 1, 3, 2, 4))
 
 

time: 51.4 us -> 48.1 us (0.936)
  local copies, waits for them, and re-layouts: 7.33 us -> 5.03 us
  Pallas kernels: 43.8 us -> 42.9 us
    unnamed x13 -> x4, local copies, waits for them, and re-layouts: 5.16 us -> 1.91 us
    pad x0 -> x1, local copies, waits for them, and re-layouts: none -> 1.07 us  [per_device(): narrow = jnp.pad(weights, ((0, 0), (0, 0), (0, window - weights.shape[2])))]
    pallas_call x1, Pallas kernels: 43.8 us -> 42.9 us  [per_device(): pl.pallas_call(functools.partial(cycle_kernel, sections, bands), out_shap...]
where the time goes in v2:
time: 48.1 us; the launch traced here: 48 us
  Pallas kernels  42.9 us (89%)
  local copies, waits for them, and re-layouts  5.03 us (10%)
    pallas_call x1, Pallas kernels, per_device(): pl.pallas_call(functools.partial(cycle_kernel, sections, bands), out_shap...  42.9 us
    transpose x1, local copies, waits for them, and re-layouts, per_device(): return jnp.transpose(result, (0, 1, 3, 2, 4))  2.05 us
    unnamed x4, local copies, waits for them, and re-layouts  1.91 us
    pad x1, local copies, waits for them, and re-layouts, per_device(): narrow = jnp.pad(weights, ((0, 0), (0, 0), (0, window - weights.shape[2])))  1.07 us

profile of v2, /device:TPU:7, one launch (start us, length us, event | category | flops | bytes accessed | tf_op | source)
XLA Modules:
  0.0 48.0 jit_solution(4350208690995821550)
XLA Ops:
  0.0 0.0 copy-start
  0.0 1.1 %pad.4.narrow = bf16[8,32,768]{2,1,0:T(8,128)(2,1)S(1)} pad(bf16[8,32,288]{2,1,0:T(8,128)(2,1)} %param.3, bf16[]{:T(256)} %constant.2.clone.1), padding=0_0x0_0x0_480 | pad | bytes 540674 | tf_op jit(solution)/shard_map/jit(_pad)/pad | solution.py:298
  1.1 1.4 %copy.14 = bf16[3,32,16,128]{3,1,2,0:T(8,128)(2,1)S(1)} copy(f32[3,32,16,128]{3,2,1,0:T(8,128)} %param.4) | data formatting | bytes 1179648 | tf_op args[1]
  2.5 0.0 copy-done
  2.5 0.5 %copy.13 = bf16[2,3,32,16,128]{4,2,3,1,0:T(8,128)(2,1)S(1)} copy(f32[2,3,32,16,128]{4,3,2,1,0:T(8,128)S(1)} %copy-done) | data formatting | bytes 2359296 | tf_op args[2]
  3.0 42.9 %shard_map.37 = f32[2,3,16,32,128]{4,3,2,1,0:T(8,128)S(1)} custom-call(bf16[8,32,768]{2,1,0:T(8,128)(2,1)S(1)} %pad.4.narrow, bf16[2,3,16,32,128]{4,3,2,1,0:T(8,128)(2,1)S(1)} %bitcast.8, bf16[3,16,32,128]{3,2,1,0:T(8,128)(2,1)S(1)} %bitcast.9), custom_call_target="tpu_custom_call" | custom-call | flops 2000000000 | bytes 8000000 | tf_op jit(solution)/shard_map/pallas_call | solution.py:304
  45.9 2.0 %copy.6 = f32[2,3,32,16,128]{4,3,2,1,0:T(8,128)} copy(f32[2,3,32,16,128]{4,2,3,1,0:T(8,128)S(1)} %bitcast.7) | data formatting | bytes 3145728 | tf_op jit(solution)/shard_map/transpose | solution.py:333
Async XLA Ops:
  0.0 2.5 %copy-start = (f32[2,3,32,16,128]{4,3,2,1,0:T(8,128)S(1)}, f32[2,3,32,16,128]{4,3,2,1,0:T(8,128)}, u32[]{:S(2)}) copy-start(f32[2,3,32,16,128]{4,3,2,1,0:T(8,128)} %param.5) | copy-start | bytes 4718596

commit v3 on v2

v3 whole, which is shorter than its diff:
```python
import functools

import jax
import jax.numpy as jnp
from jax import lax
from jax.experimental import pallas as pl
from jax.experimental.pallas import tpu as pltpu
from jax.sharding import PartitionSpec as P

M = 4
LEVELS = 2
STEP = 0.125
GROUP = 6
MESH = pl.DeviceIdType.MESH
F32 = jnp.float32
BF16 = jnp.bfloat16


def pairs(low, high):
    count = high - low
    upper = -(-count // 4)
    lower = count // 2 - upper
    middle = low + 2 * upper
    return [(low, upper, low - 1, 0), (middle, lower, middle - 1 - (GROUP - lower), GROUP - lower)]


def chunks(low, high):
    return [(start, min(start + GROUP, high)) for start in range(low, high, GROUP)]


def put(patches, start, value):
    count, channels, breadth = value.shape
    flat = value.reshape(count * channels, breadth)
    column = lax.broadcasted_iota(jnp.int32, flat.shape, 1)
    left = jnp.where(column == 0, 0.0, pltpu.roll(flat, 1, 1))
    right = jnp.where(column == breadth - 1, 0.0, pltpu.roll(flat, breadth - 1, 1))
    rows = pl.ds(start, count)
    for place, part in enumerate((left, flat, right)):
        patches[rows, place * channels : (place + 1) * channels, :] = part.reshape(value.shape).astype(BF16)


def conv(matrix_ref, layer, patches, size, window, skip):
    depth, width, breadth = patches.shape
    channels = width // 3
    parts = [
        patches[window + k * size : window + k * size + GROUP + 2].reshape((GROUP + 2) * width, breadth)
        for k in range(2)
    ]
    rows = matrix_ref[layer, skip * channels : (skip + size) * channels, :]
    product = jnp.dot(rows, jnp.concatenate(parts, axis=1), preferred_element_type=F32)
    return [
        product[:, k * breadth : (k + 1) * breadth].reshape(size, channels, breadth) for k in range(2)
    ]


def masked(value, low, first, last, above, below):
    high = low + value.shape[0]
    parts = []
    if low < first:
        parts.append(value[: min(first, high) - low] * above)
    if max(low, first) < min(high, last):
        parts.append(value[max(low, first) - low : min(high, last) - low])
    if high > last:
        parts.append(value[max(low, last) - low :] * below)
    return parts[0] if len(parts) == 1 else jnp.concatenate(parts, axis=0)


def cycle_kernel(
    sections, bands, narrow, guess, image, out,
    matrix, padded, wide0, wide1, entry, leave, state, patch, state0, patch0, defect0, defect1,
    start_send, start_recv, chain_send, chain_recv,
):
    batch, height = image.shape[0], image.shape[1]
    s = lax.axis_index("layer")
    r = lax.axis_index("rows")
    above = jnp.where(r > 0, 1.0, 0.0).astype(F32)
    below = jnp.where(r < bands - 1, 1.0, 0.0).astype(F32)
    deep0, deep1, near = M + 1, M, LEVELS

    has = {
        (i, j): functools.reduce(
            jnp.logical_and,
            [c for c in (
                s > 0 if i < 0 else (s < sections - 1 if i > 0 else None),
                r > 0 if j < 0 else (r < bands - 1 if j > 0 else None),
            ) if c is not None],
        )
        for i in (-1, 0, 1) for j in (-1, 0, 1) if (i, j) != (0, 0)
    }

    barrier = pltpu.get_barrier_semaphore()
    total = 0
    for (i, j), there in has.items():
        @pl.when(there)
        def _(i=i, j=j):
            pl.semaphore_signal(barrier, inc=1, device_id=(s + i, r + j), device_id_type=MESH)
        total = total + there.astype(jnp.int32)
    pl.semaphore_wait(barrier, total)

    def start_copy(source, target, slot, i, j):
        return pltpu.make_async_remote_copy(
            src_ref=source, dst_ref=target,
            send_sem=start_send.at[slot], recv_sem=start_recv.at[slot],
            device_id=(s + i, r + j), device_id_type=MESH,
        )

    def edge(source, wide, depth, slot, i, j):
        origin, target = (height - depth, 0) if j > 0 else (0, depth + height)
        return start_copy(
            source.at[:, pl.ds(origin, depth)], wide.at[:, pl.ds(target, depth)], slot, i, j)

    first = s == 0
    plan = [
        (edge(guess.at[0], wide1, deep1, 0, 0, 1), r < bands - 1, r > 0, 1),
        (edge(guess.at[0], wide1, deep1, 1, 0, -1), r > 0, r < bands - 1, 1),
        (start_copy(guess.at[1], wide0.at[:, pl.ds(deep0, height)], 2, 1, 0), s < sections - 1, s > 0, 0),
        (edge(guess.at[1], wide0, deep0, 3, 1, 1), has[1, 1], has[-1, -1], 0),
        (edge(guess.at[1], wide0, deep0, 4, 1, -1), has[1, -1], has[-1, 1], 0),
        (edge(image, wide0, deep0, 5, 0, 1), first & (r < bands - 1), first & (r > 0), 0),
        (edge(image, wide0, deep0, 6, 0, -1), first & (r > 0), first & (r < bands - 1), 0),
    ]
    for copy, sends, _, _ in plan:
        @pl.when(sends)
        def _(copy=copy):
            copy.start()

    @pl.when(r == 0)
    def _():
        for img in range(batch):
            wide0[img, :deep0] = jnp.zeros((deep0,) + wide0.shape[2:], BF16)
            wide1[img, :deep1] = jnp.zeros((deep1,) + wide1.shape[2:], BF16)
            entry[img, :near] = jnp.zeros((near,) + entry.shape[2:], BF16)

    @pl.when(r == bands - 1)
    def _():
        for img in range(batch):
            wide0[img, deep0 + height :] = jnp.zeros((deep0,) + wide0.shape[2:], BF16)
            wide1[img, deep1 + height :] = jnp.zeros((deep1,) + wide1.shape[2:], BF16)
            entry[img, near + height :] = jnp.zeros((near,) + entry.shape[2:], BF16)

    for img in range(batch):
        wide1[img, deep1 : deep1 + height] = guess[0, img]

    @pl.when(first)
    def _():
        for img in range(batch):
            wide0[img, deep0 : deep0 + height] = image[img]

    channels = narrow.shape[1]
    padded[...] = jnp.zeros(padded.shape, F32)
    for layer in range(narrow.shape[0]):
        padded[layer, :, : narrow.shape[2]] = narrow[layer].astype(F32)
        taps = padded[layer]
        for k in range(GROUP):
            moved = taps if k == 0 else pltpu.roll(taps, k * 3 * channels, 1)
            matrix[layer, k * channels : (k + 1) * channels, :] = moved.astype(BF16)

    def convolved(layer, patches, low, high):
        for first_row, size, window, skip in pairs(low, high):
            for k, product in enumerate(conv(matrix, layer, patches, size, window, skip)):
                yield first_row + k * size, first_row + (k + 1) * size, product

    breadth = image.shape[3]

    def lanes(img):
        return pl.ds(img * breadth, breadth)

    def relax(point):
        wide, deep, defect, extra = ((wide0, deep0, defect0, 1), (wide1, deep1, defect1, 0))[point]
        for copy, _, receives, needed in plan:
            if needed == point:
                @pl.when(receives)
                def _(copy=copy):
                    copy.wait_recv()
        end = deep + height
        for img in range(batch):
            for low, high in chunks(0, end + deep):
                value = wide[img, low:high].astype(F32)
                state[low:high, :, lanes(img)] = value
                put(patch.at[0, :, :, lanes(img)], low, value)
        for j in range(M):
            for low, high, product in convolved(point * M + j, patch.at[j % 2], j + 1, end + deep - j - 1):
                change = STEP * jnp.tanh(product)
                old = state[low:high]
                new = old + change
                a, b = max(low, deep - extra), min(high, end + extra)
                if a < b:
                    rows = pl.ds(a - deep + extra, b - a)
                    part = slice(a - low, b - low)
                    if j == 0:
                        defect[rows] = -(old + M * change)[part]
                    if j == M - 1:
                        defect[rows] = defect[rows] + new[part]
                if j < M - 1:
                    new = masked(new, low, deep, end, above, below)
                    state[low:high] = new
                    for img in range(batch):
                        own = new[:, :, img * breadth : (img + 1) * breadth]
                        put(patch.at[(j + 1) % 2, :, :, lanes(img)], low, own)

    def chain_copy(source, target, slot, img, j):
        return pltpu.make_async_remote_copy(
            src_ref=leave.at[img, source], dst_ref=entry.at[img, target],
            send_sem=chain_send.at[slot, img], recv_sem=chain_recv.at[slot, img],
            device_id=(s + 1, r + j), device_id_type=MESH,
        )

    def hand_on(img):
        return (
            (chain_copy(pl.ds(height - near, near), pl.ds(0, near), 0, img, 1), has[1, 1], has[-1, -1]),
            (chain_copy(pl.ds(0, near), pl.ds(near + height, near), 1, img, -1), has[1, -1], has[-1, 1]),
            (chain_copy(pl.ds(0, height), pl.ds(near, height), 2, img, 0), has[1, 0], has[-1, 0]),
        )

    def coarse(img):
        column = pl.ds(pl.multiple_of(img * breadth, breadth), breadth)
        for copy, _, receives in hand_on(img):
            @pl.when(receives)
            def _(copy=copy):
                copy.wait_recv()

        @pl.when(first)
        def _():
            entry[img] = wide0[img, deep0 - near : deep0 + height + near]

        end = near + height
        for low, high in chunks(0, end + near):
            value = entry[img, low:high].astype(F32)
            state0[low:high] = value
            put(patch0.at[0], low, value)
        for low, high, product in convolved(0, patch0.at[0], 1, end + 1):
            change = (M * STEP) * jnp.tanh(product)
            new = (state0[low:high] + change) + defect0[low - 1 : high - 1, :, column]
            new = masked(new, low, near, end, above, below)
            state0[low:high] = new
            put(patch0.at[1], low, new)
            a, b = max(low, near), min(high, end)
            out[0, img, a - near : b - near] = new[a - low : b - low]
        for low, high, product in convolved(M, patch0.at[1], near, end):
            change = (M * STEP) * jnp.tanh(product)
            rows = slice(low - near, high - near)
            new = (state0[low:high] + change) + defect1[rows, :, column]
            out[1, img, rows] = new
            leave[img, rows] = new.astype(BF16)
        for copy, sends, _ in hand_on(img):
            @pl.when(sends)
            def _(copy=copy):
                copy.start()

    for point in range(LEVELS - 1, -1, -1):
        relax(point)

    def link(img, carry):
        coarse(img)
        return carry

    lax.fori_loop(0, batch, link, 0)

    for copy, sends, _, _ in plan:
        @pl.when(sends)
        def _(copy=copy):
            copy.wait_send()

    for img in range(batch):
        for copy, sends, _ in hand_on(img):
            @pl.when(sends)
            def _(copy=copy):
                copy.wait_send()


def per_device(sections, bands, weights, image, guess):
    levels, batch, channels, height, breadth = guess.shape
    window = (GROUP + 2) * 3 * channels
    moved = jnp.transpose(guess, (0, 1, 3, 2, 4)).astype(BF16)
    picture = jnp.transpose(image, (0, 2, 1, 3)).astype(BF16)
    rows0, rows1 = height + 2 * (M + 1), height + 2 * M
    plane = (channels, breadth)
    wide_plane = (3 * channels, breadth)
    result = pl.pallas_call(
        functools.partial(cycle_kernel, sections, bands),
        out_shape=jax.ShapeDtypeStruct((levels, batch, height) + plane, F32),
        in_specs=[pl.BlockSpec(memory_space=pltpu.VMEM)] * 3,
        out_specs=pl.BlockSpec(memory_space=pltpu.VMEM),
        scratch_shapes=[
            pltpu.VMEM((weights.shape[0], GROUP * channels, window), BF16),
            pltpu.VMEM((weights.shape[0], channels, window), F32),
            pltpu.VMEM((batch, rows0) + plane, BF16),
            pltpu.VMEM((batch, rows1) + plane, BF16),
            pltpu.VMEM((batch, height + 2 * LEVELS) + plane, BF16),
            pltpu.VMEM((batch, height) + plane, BF16),
            pltpu.VMEM((rows0, channels, batch * breadth), F32),
            pltpu.VMEM((2, rows0, 3 * channels, batch * breadth), BF16),
            pltpu.VMEM((height + 2 * LEVELS,) + plane, F32),
            pltpu.VMEM((2, height + 2 * LEVELS) + wide_plane, BF16),
            pltpu.VMEM((height + 2, channels, batch * breadth), F32),
            pltpu.VMEM((height, channels, batch * breadth), F32),
            pltpu.SemaphoreType.DMA((7,)),
            pltpu.SemaphoreType.DMA((7,)),
            pltpu.SemaphoreType.DMA((3, batch)),
            pltpu.SemaphoreType.DMA((3, batch)),
        ],
        compiler_params=pltpu.CompilerParams(
            collective_id=0, has_side_effects=True, vmem_limit_bytes=40 * 1024 * 1024
        ),
        cost_estimate=pl.CostEstimate(
            flops=2_000_000_000, bytes_accessed=8_000_000, transcendentals=2_500_000
        ),
    )(weights, moved, picture)
    return jnp.transpose(result, (0, 1, 3, 2, 4))


def solution(mesh):
    sizes = dict(mesh.shape)
    return jax.shard_map(
        functools.partial(per_device, sizes["layer"], sizes["rows"]),
        mesh=mesh,
        in_specs=(
            P("layer", None, None),
            P(None, None, "rows", None),
            P("layer", None, None, "rows", None),
        ),
        out_specs=P("layer", None, None, "rows", None),
        check_vma=False,
    )
```

time: 48.1 us -> 49.9 us (1.037)
  Pallas kernels: 42.9 us -> 44.3 us
    unnamed x4, local copies, waits for them, and re-layouts: 1.91 us -> 3.35 us
    pallas_call x1, Pallas kernels: 42.9 us -> 44.3 us  [per_device(): pl.pallas_call(functools.partial(cycle_kernel, sections, bands), out_shap...]
    pad x1 -> x0, local copies, waits for them, and re-layouts: 1.07 us -> none  [per_device(): narrow = jnp.pad(weights, ((0, 0), (0, 0), (0, window - weights.shape[2])))]
where the time goes in v3:
time: 49.9 us; the launch traced here: 49.7 us
  Pallas kernels  44.3 us (89%)
  local copies, waits for them, and re-layouts  5.4 us (11%)
    pallas_call x1, Pallas kernels, per_device(): pl.pallas_call(functools.partial(cycle_kernel, sections, bands), out_shap...  44.3 us
    unnamed x4, local copies, waits for them, and re-layouts  3.35 us
    transpose x1, local copies, waits for them, and re-layouts, per_device(): return jnp.transpose(result, (0, 1, 3, 2, 4))  2.05 us

profile of v3, /device:TPU:7, one launch (start us, length us, event | category | flops | bytes accessed | tf_op | source)
XLA Modules:
  0.0 49.7 jit_solution(16287490927014343406)
XLA Ops:
  0.0 0.0 copy-start
  0.0 1.4 %copy.14 = bf16[3,32,16,128]{3,1,2,0:T(8,128)(2,1)S(1)} copy(f32[3,32,16,128]{3,2,1,0:T(8,128)} %param.4) | data formatting | bytes 1179648 | tf_op args[1]
  1.4 1.9 %copy.13 = bf16[2,3,32,16,128]{4,2,3,1,0:T(8,128)(2,1)S(1)} copy(f32[2,3,32,16,128]{4,3,2,1,0:T(8,128)} %param.5) | data formatting | bytes 2359296 | tf_op args[2]
  3.4 0.0 copy-done
  3.4 44.3 %shard_map.37 = f32[2,3,16,32,128]{4,3,2,1,0:T(8,128)S(1)} custom-call(bf16[8,32,288]{2,1,0:T(8,128)(2,1)S(1)} %copy-done, bf16[2,3,16,32,128]{4,3,2,1,0:T(8,128)(2,1)S(1)} %bitcast.8, bf16[3,16,32,128]{3,2,1,0:T(8,128)(2,1)S(1)} %bitcast.9), custom_call_target="tpu_custom_call" | custom-call | flops 2000000000 | bytes 8000000 | tf_op jit(solution)/shard_map/pallas_call | solution.py:279
  47.7 2.0 %copy.6 = f32[2,3,32,16,128]{4,3,2,1,0:T(8,128)} copy(f32[2,3,32,16,128]{4,2,3,1,0:T(8,128)S(1)} %bitcast.7) | data formatting | bytes 3145728 | tf_op jit(solution)/shard_map/transpose | solution.py:309
Async XLA Ops:
  0.0 3.4 %copy-start = (bf16[8,32,288]{2,1,0:T(8,128)(2,1)S(1)}, bf16[8,32,288]{2,1,0:T(8,128)(2,1)}, u32[]{:S(2)}) copy-start(bf16[8,32,288]{2,1,0:T(8,128)(2,1)} %narrow.1) | copy-start | bytes 442372

commit v4 on v2

--- a/solution.py
+++ b/solution.py
@@ -28,29 +28,27 @@
     return [(start, min(start + GROUP, high)) for start in range(low, high, GROUP)]
 
 
-def put(patches, start, value):
-    count, channels, breadth = value.shape
-    flat = value.reshape(count * channels, breadth)
-    column = lax.broadcasted_iota(jnp.int32, flat.shape, 1)
-    left = jnp.where(column == 0, 0.0, pltpu.roll(flat, 1, 1))
-    right = jnp.where(column == breadth - 1, 0.0, pltpu.roll(flat, breadth - 1, 1))
-    rows = pl.ds(start, count)
-    for place, part in enumerate((left, flat, right)):
-        patches[rows, place * channels : (place + 1) * channels, :] = part.reshape(value.shape).astype(BF16)
-
-
-def conv(matrix_ref, layer, patches, size, window, skip):
-    depth, width, breadth = patches.shape
-    channels = width // 3
+def conv(matrix_ref, layer, state, size, window, skip):
+    channels, breadth = state.shape[1:]
     parts = [
-        patches[window + k * size : window + k * size + GROUP + 2].reshape((GROUP + 2) * width, breadth)
+        state[window + k * size : window + k * size + GROUP + 2].reshape((GROUP + 2) * channels, breadth)
         for k in range(2)
     ]
-    rows = matrix_ref[layer, skip * channels : (skip + size) * channels, :]
-    product = jnp.dot(rows, jnp.concatenate(parts, axis=1), preferred_element_type=F32)
-    return [
-        product[:, k * breadth : (k + 1) * breadth].reshape(size, channels, breadth) for k in range(2)
-    ]
+    count = size * channels
+    rows = [matrix_ref[layer, tap, skip * channels : skip * channels + count, :] for tap in range(3)]
+    product = jnp.dot(
+        jnp.concatenate(rows, axis=0), jnp.concatenate(parts, axis=1), preferred_element_type=F32
+    )
+    column = lax.broadcasted_iota(jnp.int32, (count, breadth), 1)
+    results = []
+    for k in range(2):
+        left, middle, right = (
+            product[tap * count : (tap + 1) * count, k * breadth : (k + 1) * breadth] for tap in range(3)
+        )
+        left = jnp.where(column == 0, 0.0, pltpu.roll(left, 1, 1))
+        right = jnp.where(column == breadth - 1, 0.0, pltpu.roll(right, breadth - 1, 1))
+        results.append((left + middle + right).reshape(size, channels, breadth))
+    return results
 
 
 def masked(value, low, first, last, above, below):
@@ -165,12 +163,13 @@
         for img in range(batch):
             wide0[img, deep0 : deep0 + height] = image[img]
 
-    channels = narrow.shape[1]
+    channels = narrow.shape[2]
     for layer in range(narrow.shape[0]):
-        taps = narrow[layer].astype(F32)
-        for k in range(GROUP):
-            moved = taps if k == 0 else pltpu.roll(taps, k * 3 * channels, 1)
-            matrix[layer, k * channels : (k + 1) * channels, :] = moved.astype(BF16)
+        for tap in range(3):
+            taps = narrow[layer, tap].astype(F32)
+            for k in range(GROUP):
+                moved = taps if k == 0 else pltpu.roll(taps, k * channels, 1)
+                matrix[layer, tap, k * channels : (k + 1) * channels, :] = moved.astype(BF16)
 
     def convolved(layer, patches, low, high):
         for first_row, size, window, skip in pairs(low, high):
@@ -190,7 +189,7 @@
             for low, high in chunks(0, height + 2 * deep):
                 value = wide[img, low:high].astype(F32)
                 state[low:high] = value
-                put(patch.at[0], low, value)
+                patch[0, low:high] = value.astype(BF16)
         for j in range(M):
             for point, _, deep, state, patch, defect, extra in anchors:
                 end = deep + height
@@ -209,7 +208,7 @@
                     if j < M - 1:
                         new = masked(new, low, deep, end, above, below)
                         state[low:high] = new
-                        put(patch.at[(j + 1) % 2], low, new)
+                        patch[(j + 1) % 2, low:high] = new.astype(BF16)
 
     def chain_copy(source, target, slot, img, j):
         return pltpu.make_async_remote_copy(
@@ -242,17 +241,17 @@
         for low, high in chunks(0, end + near):
             value = entry[img, low:high].astype(F32)
             state0[low:high] = value
-            put(patch0.at[0], low, value)
+            patch0[0, low:high] = entry[img, low:high]
         for low, high, product in convolved(0, patch0.at[0], 1, end + 1):
             change = (M * STEP) * jnp.tanh(product)
             new = (state0[low:high] + change) + defect0[img, low - 1 : high - 1]
             new = masked(new, low, near, end, above, below)
             state0[low:high] = new
-            put(patch0.at[1], low, new)
+            patch0[1, low:high] = new.astype(BF16)
             a, b = max(low, near), min(high, end)
             out[0, img, a - near : b - near] = new[a - low : b - low]
         ready = list(hand_on(img))
-        for low, high, product in convolved(M, patch0.at[1], near, end):
+        for low, high, product in list(convolved(M, patch0.at[1], near, end)):
             change = (M * STEP) * jnp.tanh(product)
             rows = slice(low - near, high - near)
             new = (state0[low:high] + change) + defect1[img, rows]
@@ -294,28 +293,29 @@
 
 def per_device(sections, bands, weights, image, guess):
     levels, batch, channels, height, breadth = guess.shape
-    window = (GROUP + 2) * 3 * channels
-    narrow = jnp.pad(weights, ((0, 0), (0, 0), (0, window - weights.shape[2])))
+    window = (GROUP + 2) * channels
+    narrow = weights.reshape(weights.shape[0], channels, 3, 3, channels)
+    narrow = jnp.transpose(narrow, (0, 3, 1, 2, 4)).reshape(weights.shape[0], 3, channels, 3 * channels)
+    narrow = jnp.pad(narrow, ((0, 0), (0, 0), (0, 0), (0, window - 3 * channels)))
     moved = jnp.transpose(guess, (0, 1, 3, 2, 4)).astype(BF16)
     picture = jnp.transpose(image, (0, 2, 1, 3)).astype(BF16)
     rows0, rows1 = height + 2 * (M + 1), height + 2 * M
     plane = (channels, breadth)
-    wide_plane = (3 * channels, breadth)
     result = pl.pallas_call(
         functools.partial(cycle_kernel, sections, bands),
         out_shape=jax.ShapeDtypeStruct((levels, batch, height) + plane, F32),
         in_specs=[pl.BlockSpec(memory_space=pltpu.VMEM)] * 3,
         out_specs=pl.BlockSpec(memory_space=pltpu.VMEM),
         scratch_shapes=[
-            pltpu.VMEM((weights.shape[0], GROUP * channels, window), BF16),
+            pltpu.VMEM((weights.shape[0], 3, GROUP * channels, window), BF16),
             pltpu.VMEM((batch, rows0) + plane, BF16),
             pltpu.VMEM((batch, rows1) + plane, BF16),
             pltpu.VMEM((batch, height + 2 * LEVELS) + plane, BF16),
             pltpu.VMEM((batch, height) + plane, BF16),
             pltpu.VMEM((rows0,) + plane, F32),
             pltpu.VMEM((rows1,) + plane, F32),
-            pltpu.VMEM((2, rows0) + wide_plane, BF16),
-            pltpu.VMEM((2, rows1) + wide_plane, BF16),
+            pltpu.VMEM((2, rows0) + plane, BF16),
+            pltpu.VMEM((2, rows1) + plane, BF16),
             pltpu.VMEM((batch, height + 2) + plane, F32),
             pltpu.VMEM((batch, height) + plane, F32),
             pltpu.SemaphoreType.DMA((7, batch)),

time: 48.1 us -> 50.3 us (1.046)
  local copies, waits for them, and re-layouts: 5.03 us -> 6.97 us
    reshape x0 -> x2, local copies, waits for them, and re-layouts: none -> 1.97 us  [the longest x1 1.64 us: per_device(): narrow = weights.reshape(weights.shape[0], channels, 3, 3, channels)]
    pad x1, local copies, waits for them, and re-layouts: 1.07 us -> 0.07 us  [per_device(): jnp.pad(narrow, ((0, 0), (0, 0), (0, 0), (0, window - 3 * channels)))]
    unnamed x4, local copies, waits for them, and re-layouts: 1.91 us -> 2.45 us
where the time goes in v4:
time: 50.3 us; the launch traced here: 50.1 us
  Pallas kernels  43.1 us (86%)
  local copies, waits for them, and re-layouts  6.97 us (14%)
    pallas_call x1, Pallas kernels, per_device(): pl.pallas_call(functools.partial(cycle_kernel, sections, bands), out_shap...  43.1 us
    unnamed x4, local copies, waits for them, and re-layouts  2.45 us
    transpose x1, local copies, waits for them, and re-layouts, per_device(): return jnp.transpose(result, (0, 1, 3, 2, 4))  2.05 us
    reshape x1, local copies, waits for them, and re-layouts, per_device(): narrow = weights.reshape(weights.shape[0], channels, 3, 3, channels)  1.64 us

profile of v4, /device:TPU:7, one launch (start us, length us, event | category | flops | bytes accessed | tf_op | source)
XLA Modules:
  0.0 50.1 jit_solution(16753868084311049002)
XLA Ops:
  0.0 1.4 %copy.19 = bf16[3,32,16,128]{3,1,2,0:T(8,128)(2,1)S(1)} copy(f32[3,32,16,128]{3,2,1,0:T(8,128)} %param.4) | data formatting | bytes 1179648 | tf_op args[1]
  1.4 1.6 %reshape.6 = bf16[8,32,3,3,32]{4,3,2,1,0:T(4,128)(2,1)S(1)} reshape(bf16[8,32,288]{2,1,0:T(8,128)(2,1)} %param.3) | data formatting | bytes 294912 | tf_op jit(solution)/shard_map/reshape | solution.py:297
  3.0 0.0 copy-start
  3.1 0.4 copy.8
  3.5 0.3 reshape.7
  3.8 0.1 pad.4.narrow
  3.9 0.5 %copy-done = f32[2,3,32,16,128]{4,3,2,1,0:T(8,128)S(1)} copy-done((f32[2,3,32,16,128]{4,3,2,1,0:T(8,128)S(1)}, f32[2,3,32,16,128]{4,3,2,1,0:T(8,128)}, u32[]{:S(2)}) %copy-start) | copy-done | bytes 1572888
  4.5 0.5 %copy.18 = bf16[2,3,32,16,128]{4,2,3,1,0:T(8,128)(2,1)S(1)} copy(f32[2,3,32,16,128]{4,3,2,1,0:T(8,128)S(1)} %copy-done) | data formatting | bytes 2359296 | tf_op args[2]
  5.0 43.1 %shard_map.37 = f32[2,3,16,32,128]{4,3,2,1,0:T(8,128)S(1)} custom-call(bf16[8,3,32,256]{3,2,1,0:T(8,128)(2,1)S(1)} %pad.4.narrow, bf16[2,3,16,32,128]{4,3,2,1,0:T(8,128)(2,1)S(1)} %bitcast.9, bf16[3,16,32,128]{3,2,1,0:T(8,128)(2,1)S(1)} %bitcast.10), custom_call_target="tpu_custom_call" | custom-call | flops 2000000000 | bytes 8000000 | tf_op jit(solution)/shard_map/pallas_call | solution.py:304
  48.0 2.0 %copy.11 = f32[2,3,32,16,128]{4,3,2,1,0:T(8,128)} copy(f32[2,3,32,16,128]{4,2,3,1,0:T(8,128)S(1)} %bitcast.8) | data formatting | bytes 3145728 | tf_op jit(solution)/shard_map/transpose | solution.py:333
Async XLA Ops:
  3.0 1.4 %copy-start = (f32[2,3,32,16,128]{4,3,2,1,0:T(8,128)S(1)}, f32[2,3,32,16,128]{4,3,2,1,0:T(8,128)}, u32[]{:S(2)}) copy-start(f32[2,3,32,16,128]{4,3,2,1,0:T(8,128)} %param.5) | copy-start | bytes 4718596

commit v5 on v2

--- a/solution.py
+++ b/solution.py
@@ -137,11 +137,18 @@
         (down1, r < bands - 1, r > 0),
         (up1, r > 0, r < bands - 1),
     ]
-    for img in range(batch):
-        for copy, sends, _ in plan:
-            @pl.when(sends)
-            def _(img=img, copy=copy):
-                copy(img).start()
+    urgent, band, slanted = plan[1:3] + plan[5:], plan[:1], plan[3:5]
+
+    def send(chosen, unless=None):
+        for img in range(batch):
+            for copy, sends, _ in chosen:
+                @pl.when(sends if unless is None else sends & unless)
+                def _(img=img, copy=copy):
+                    copy(img).start()
+
+    send(urgent)
+    send(band)
+    send(slanted, jnp.logical_not(first))
 
     @pl.when(r == 0)
     def _():
@@ -276,6 +283,10 @@
         @pl.when(jnp.logical_not(relaxes))
         def _():
             coarse(img)
+
+        @pl.when(first & (t == 0))
+        def _():
+            send(slanted)
 
         return carry
 

time: 48.1 us -> 50.3 us (1.046)
  Pallas kernels: 42.9 us -> 45.1 us
    pallas_call x1, Pallas kernels: 42.9 us -> 45.1 us  [per_device(): pl.pallas_call(functools.partial(cycle_kernel, sections, bands), out_shap...]
where the time goes in v5:
time: 50.3 us; the launch traced here: 50.1 us
  Pallas kernels  45.1 us (90%)
  local copies, waits for them, and re-layouts  5.03 us (10%)
    pallas_call x1, Pallas kernels, per_device(): pl.pallas_call(functools.partial(cycle_kernel, sections, bands), out_shap...  45.1 us
    transpose x1, local copies, waits for them, and re-layouts, per_device(): return jnp.transpose(result, (0, 1, 3, 2, 4))  2.05 us
    unnamed x4, local copies, waits for them, and re-layouts  1.91 us
    pad x1, local copies, waits for them, and re-layouts, per_device(): narrow = jnp.pad(weights, ((0, 0), (0, 0), (0, window - weights.shape[2])))  1.07 us

profile of v5, /device:TPU:7, one launch (start us, length us, event | category | flops | bytes accessed | tf_op | source)
XLA Modules:
  0.0 50.1 jit_solution(11286762059259889425)
XLA Ops:
  0.0 0.0 copy-start
  0.0 1.1 %pad.4.narrow = bf16[8,32,768]{2,1,0:T(8,128)(2,1)S(1)} pad(bf16[8,32,288]{2,1,0:T(8,128)(2,1)} %param.3, bf16[]{:T(256)} %constant.2.clone.1), padding=0_0x0_0x0_480 | pad | bytes 540674 | tf_op jit(solution)/shard_map/jit(_pad)/pad | solution.py:309
  1.1 1.4 %copy.14 = bf16[3,32,16,128]{3,1,2,0:T(8,128)(2,1)S(1)} copy(f32[3,32,16,128]{3,2,1,0:T(8,128)} %param.4) | data formatting | bytes 1179648 | tf_op args[1]
  2.5 0.0 copy-done
  2.5 0.5 %copy.13 = bf16[2,3,32,16,128]{4,2,3,1,0:T(8,128)(2,1)S(1)} copy(f32[2,3,32,16,128]{4,3,2,1,0:T(8,128)S(1)} %copy-done) | data formatting | bytes 2359296 | tf_op args[2]
  3.0 45.1 %shard_map.37 = f32[2,3,16,32,128]{4,3,2,1,0:T(8,128)S(1)} custom-call(bf16[8,32,768]{2,1,0:T(8,128)(2,1)S(1)} %pad.4.narrow, bf16[2,3,16,32,128]{4,3,2,1,0:T(8,128)(2,1)S(1)} %bitcast.8, bf16[3,16,32,128]{3,2,1,0:T(8,128)(2,1)S(1)} %bitcast.9), custom_call_target="tpu_custom_call" | custom-call | flops 2000000000 | bytes 8000000 | tf_op jit(solution)/shard_map/pallas_call | solution.py:315
  48.1 2.0 %copy.6 = f32[2,3,32,16,128]{4,3,2,1,0:T(8,128)} copy(f32[2,3,32,16,128]{4,2,3,1,0:T(8,128)S(1)} %bitcast.7) | data formatting | bytes 3145728 | tf_op jit(solution)/shard_map/transpose | solution.py:344
Async XLA Ops:
  0.0 2.5 %copy-start = (f32[2,3,32,16,128]{4,3,2,1,0:T(8,128)S(1)}, f32[2,3,32,16,128]{4,3,2,1,0:T(8,128)}, u32[]{:S(2)}) copy-start(f32[2,3,32,16,128]{4,3,2,1,0:T(8,128)} %param.5) | copy-start | bytes 4718596

commit v6 on v2

--- a/solution.py
+++ b/solution.py
@@ -165,12 +165,20 @@
         for img in range(batch):
             wide0[img, deep0 : deep0 + height] = image[img]
 
-    channels = narrow.shape[1]
+    channels, reach = narrow.shape[1:]
+    whole = matrix.shape[2]
+    tile = 128
     for layer in range(narrow.shape[0]):
         taps = narrow[layer].astype(F32)
         for k in range(GROUP):
-            moved = taps if k == 0 else pltpu.roll(taps, k * 3 * channels, 1)
-            matrix[layer, k * channels : (k + 1) * channels, :] = moved.astype(BF16)
+            whole_tiles, rest = divmod(k * 3 * channels, tile)
+            origin = whole_tiles * tile
+            moved = (pltpu.roll(taps, rest, 1) if rest else taps).astype(BF16)
+            parts = [jnp.zeros((channels, origin), BF16)] if origin else []
+            parts.append(moved)
+            if origin + reach < whole:
+                parts.append(jnp.zeros((channels, whole - origin - reach), BF16))
+            matrix[layer, k * channels : (k + 1) * channels, :] = jnp.concatenate(parts, axis=1)
 
     def convolved(layer, patches, low, high):
         for first_row, size, window, skip in pairs(low, high):
@@ -295,7 +303,7 @@
 def per_device(sections, bands, weights, image, guess):
     levels, batch, channels, height, breadth = guess.shape
     window = (GROUP + 2) * 3 * channels
-    narrow = jnp.pad(weights, ((0, 0), (0, 0), (0, window - weights.shape[2])))
+    narrow = jnp.pad(weights, ((0, 0), (0, 0), (0, 3 * channels)))
     moved = jnp.transpose(guess, (0, 1, 3, 2, 4)).astype(BF16)
     picture = jnp.transpose(image, (0, 2, 1, 3)).astype(BF16)
     rows0, rows1 = height + 2 * (M + 1), height + 2 * M

time: 48.1 us -> 48.1 us (level)
  no operation moved by 1% of the time
where the time goes in v6:
time: 48.1 us; the launch traced here: 47.9 us
  Pallas kernels  42.9 us (89%)
  local copies, waits for them, and re-layouts  5.02 us (10%)
    pallas_call x1, Pallas kernels, per_device(): pl.pallas_call(functools.partial(cycle_kernel, sections, bands), out_shap...  42.9 us
    transpose x1, local copies, waits for them, and re-layouts, per_device(): return jnp.transpose(result, (0, 1, 3, 2, 4))  2.05 us
    unnamed x4, local copies, waits for them, and re-layouts  1.91 us
    pad x1, local copies, waits for them, and re-layouts, per_device(): narrow = jnp.pad(weights, ((0, 0), (0, 0), (0, 3 * channels)))  1.07 us

profile of v6, /device:TPU:7, one launch (start us, length us, event | category | flops | bytes accessed | tf_op | source)
XLA Modules:
  0.0 47.9 jit_solution(6279322070432488217)
XLA Ops:
  0.0 0.0 copy-start
  0.0 1.1 %pad.4.narrow = bf16[8,32,384]{2,1,0:T(8,128)(2,1)S(1)} pad(bf16[8,32,288]{2,1,0:T(8,128)(2,1)} %param.3, bf16[]{:T(256)} %constant.2.clone.1), padding=0_0x0_0x0_96 | pad | bytes 344066 | tf_op jit(solution)/shard_map/jit(_pad)/pad | solution.py:306
  1.1 1.4 %copy.14 = bf16[3,32,16,128]{3,1,2,0:T(8,128)(2,1)S(1)} copy(f32[3,32,16,128]{3,2,1,0:T(8,128)} %param.4) | data formatting | bytes 1179648 | tf_op args[1]
  2.5 0.0 copy-done
  2.5 0.5 %copy.13 = bf16[2,3,32,16,128]{4,2,3,1,0:T(8,128)(2,1)S(1)} copy(f32[2,3,32,16,128]{4,3,2,1,0:T(8,128)S(1)} %copy-done) | data formatting | bytes 2359296 | tf_op args[2]
  3.0 42.9 %shard_map.37 = f32[2,3,16,32,128]{4,3,2,1,0:T(8,128)S(1)} custom-call(bf16[8,32,384]{2,1,0:T(8,128)(2,1)S(1)} %pad.4.narrow, bf16[2,3,16,32,128]{4,3,2,1,0:T(8,128)(2,1)S(1)} %bitcast.8, bf16[3,16,32,128]{3,2,1,0:T(8,128)(2,1)S(1)} %bitcast.9), custom_call_target="tpu_custom_call" | custom-call | flops 2000000000 | bytes 8000000 | tf_op jit(solution)/shard_map/pallas_call | solution.py:312
  45.9 2.0 %copy.6 = f32[2,3,32,16,128]{4,3,2,1,0:T(8,128)} copy(f32[2,3,32,16,128]{4,2,3,1,0:T(8,128)S(1)} %bitcast.7) | data formatting | bytes 3145728 | tf_op jit(solution)/shard_map/transpose | solution.py:341
Async XLA Ops:
  0.0 2.5 %copy-start = (f32[2,3,32,16,128]{4,3,2,1,0:T(8,128)S(1)}, f32[2,3,32,16,128]{4,3,2,1,0:T(8,128)}, u32[]{:S(2)}) copy-start(f32[2,3,32,16,128]{4,3,2,1,0:T(8,128)} %param.5) | copy-start | bytes 4718596
